TPU v7x, 512 devices: a whole 4x4x16 slice. The times are simulated.
512 devices in a mesh: space: 64 (over x, z), tile: 8 (over y, core).
Axes of the slice: x: 4, y: 4, z: 16, core: 2. Of those that a mesh axis runs over, the one named last changes fastest.
Arguments:
- features: bfloat16 [512, 64, 8, 128], P('space', 'tile'), may hold values from -6 to 6
- occupancy: int32 [512, 64, 8], P('space', 'tile'), may hold values 0 or 1
- kernel: bfloat16 [27, 128, 128], replicated, may hold values from -0.109375 to 0.109375
- cotangent: bfloat16 [512, 64, 8, 128], P('space', 'tile'), may hold values from -6 to 6
Outputs:
- outputs: bfloat16 [512, 64, 8, 128], P('space', 'tile')
- feature_grad: bfloat16 [512, 64, 8, 128], P('space', 'tile')
- kernel_grad: float32 [27, 128, 128], replicated
All inputs are finite; a program needn't handle non-finite values. No bound on the sum of `occupancy` on one device may be relied on, other than what follows from the above.
Results may differ from a plain program's by a relative error of at most 0.001.
Values may be sent and summed in bfloat16 or wider, within the bound.
A program may use at most 64 MiB of HBM per device.

v0:
```python
import math

import jax
import jax.numpy as jnp
from jax import lax
from jax.sharding import PartitionSpec as P


def extended(x, sides, width):
    for axis, dim in sides:
        devices, length = (lax.axis_size(axis), x.shape[dim])
        up = [(i, (i + 1) % devices) for i in range(devices - 1)]
        down = [(j, i) for i, j in up]
        last = lax.slice_in_dim(x, length - width, length, axis=dim)
        initial = lax.slice_in_dim(x, 0, width, axis=dim)
        before = lax.ppermute(last, axis, up)
        after = lax.ppermute(initial, axis, down)
        x = jnp.concatenate([before, x, after], axis=dim)
    return x


def convolve(padded, weight):
    size_x = padded.shape[0] - 2
    size_y = padded.shape[1] - 2
    size_z = padded.shape[2] - 2
    width_out = weight.shape[2]
    total = jnp.zeros((size_x * size_y * size_z, width_out), jnp.float32)
    for shift_x in range(3):
        for shift_y in range(3):
            stacked = jnp.concatenate(
                [
                    padded[
                        shift_x : shift_x + size_x,
                        shift_y : shift_y + size_y,
                        shift_z : shift_z + size_z,
                        :,
                    ]
                    for shift_z in range(3)
                ],
                axis=-1,
            )
            stacked = stacked.reshape(size_x * size_y * size_z, -1)
            first = 9 * shift_x + 3 * shift_y
            total = total + jnp.dot(
                stacked,
                weight[first : first + 3].reshape(-1, width_out),
                preferred_element_type=jnp.float32,
            )
    return total.reshape(size_x, size_y, size_z, width_out)


def kernel_terms(padded, grads):
    size_x, size_y, size_z, width = grads.shape
    flat_grads = grads.reshape(size_x * size_y * size_z, width)
    pieces = []
    for shift_x in range(3):
        for shift_y in range(3):
            stacked = jnp.concatenate(
                [
                    padded[
                        shift_x : shift_x + size_x,
                        shift_y : shift_y + size_y,
                        shift_z : shift_z + size_z,
                        :,
                    ]
                    for shift_z in range(3)
                ],
                axis=-1,
            )
            stacked = stacked.reshape(size_x * size_y * size_z, -1)
            product = lax.dot_general(
                stacked, flat_grads, (((0,), (0,)), ((), ())), preferred_element_type=jnp.float32
            )
            pieces.append(product.reshape(3, width, width))
    return jnp.concatenate(pieces, axis=0)


def shards(features, occupancy, kernel, cotangent):
    mask_low = occupancy.astype(jnp.bfloat16)[..., None]
    mask_full = occupancy.astype(jnp.float32)[..., None]
    masked = features * mask_low
    masked_grad = cotangent * mask_low
    padded = extended(masked, (("space", 0), ("tile", 1)), 1)
    padded = jnp.pad(padded, ((0, 0), (0, 0), (1, 1), (0, 0)))
    padded_grad = extended(masked_grad, (("space", 0), ("tile", 1)), 1)
    padded_grad = jnp.pad(padded_grad, ((0, 0), (0, 0), (1, 1), (0, 0)))
    outputs = (convolve(padded, kernel) * mask_full).astype(jnp.bfloat16)
    flipped = jnp.transpose(kernel[::-1], (0, 2, 1))
    feature_grad = (convolve(padded_grad, flipped) * mask_full).astype(jnp.bfloat16)
    local_term = kernel_terms(padded, masked_grad)
    voxels = (
        features.shape[0]
        * features.shape[1]
        * features.shape[2]
        * lax.axis_size("space")
        * lax.axis_size("tile")
    )
    scale = 1.0 / math.sqrt(voxels)
    kernel_grad = lax.psum(local_term, ("space", "tile")) * scale
    return (outputs, feature_grad, kernel_grad)


def solution(mesh):
    in_specs = (
        P("space", "tile", None, None),
        P("space", "tile", None),
        P(),
        P("space", "tile", None, None),
    )
    out_specs = (P("space", "tile", None, None), P("space", "tile", None, None), P())
    return jax.shard_map(shards, mesh=mesh, in_specs=in_specs, out_specs=out_specs, check_vma=False)
```

profile of v0, /device:TPU:1, one launch (start us, length us, event | category | flops | bytes accessed | tf_op | source)
XLA Modules:
  0.0 556.2 jit_solution(1008610432489222102)
XLA Ops:
  7.2 1.4 fusion.24
  8.7 1.1 broadcast_multiply_fusion.1
  9.8 1.3 collective-permute-start.5
  11.1 5.0 collective-permute-start.4
  16.1 1.3 collective-permute-start.1
  17.4 4.2 collective-permute-start
  21.6 1.9 copy.16
  23.5 1.0 fusion.15
  24.5 1.0 fusion.14
  25.6 8.7 %collective-permute-start.7 = (bf16[10,1,8,128]{3,2,1,0:T(8,128)(2,1)S(1)}, bf16[10,1,8,128]{3,2,1,0:T(8,128)(2,1)S(1)}, u32[]{:S(2)}, u32[]{:S(2)}) collective-permute-start(bf16[10,1,8,128]{3,2,1,0:T(8,128)(2,1)S(1)} %get-tuple-element.72), channel_id=1, source_target_pairs={{1,0},{2,1},{3,2},{4,3},{5,4},{6,5},{7,6},{9,8},{10,9},{11,10},{12... | collective-permute-start | bytes 61448 | tf_op jit(solution)/shard_map/ppermute | solution.py:17
  34.3 1.9 collective-permute-start.6
  36.3 2.4 collective-permute-start.3
  38.7 3.2 collective-permute-start.2
  41.9 0.2 select_maximum_fusion
  42.1 1.4 fusion.16
  43.6 0.8 fusion.19
  44.5 0.8 fusion.18
  45.3 0.2 select_maximum_fusion.4
  45.5 1.1 fusion.17
  46.8 0.8 fusion.21
  47.6 0.8 fusion.20
  48.4 0.9 copy.17
  49.4 0.3 fusion.25
  49.7 0.9 fusion.11
  50.5 0.9 copy.18
  51.5 1.0 copy.19
  52.5 1.1 pad_maximum_fusion.6
  53.5 0.9 copy.20
  54.5 0.9 copy.21
  55.4 0.9 copy.22
  56.3 1.3 pad_maximum_fusion.9
  57.7 0.9 copy.23
  58.6 0.9 copy.24
  59.5 0.9 copy.25
  60.5 2.0 convolution_dynamic-update-slice_fusion.8
  62.5 2.0 convolution_dynamic-update-slice_fusion.7
  64.5 2.0 convolution_dynamic-update-slice_fusion.6
  66.5 0.9 convolution_dynamic-update-slice_fusion.5
  67.4 0.9 convolution_dynamic-update-slice_fusion.4
  68.4 0.9 convolution_dynamic-update-slice_fusion.3
  69.3 0.9 convolution_dynamic-update-slice_fusion.2
  70.3 0.9 convolution_dynamic-update-slice_fusion.1
  71.2 0.9 convolution_dynamic-update-slice_fusion
  72.2 1.3 pad_maximum_fusion.11
  73.6 1.2 fusion.26
  74.8 0.3 convolution_add_fusion.15
  75.1 0.3 convolution_add_fusion.14
  75.3 0.3 convolution_add_fusion.13
  75.6 0.3 convolution_add_fusion.12
  75.9 0.3 convolution_add_fusion.11
  76.3 0.3 convolution_add_fusion.10
  76.6 0.3 convolution_add_fusion.9
  76.9 0.3 convolution_add_fusion.8
  77.8 0.3 convolution_add_fusion.7
  78.1 0.3 convolution_add_fusion.6
  78.8 0.3 convolution_add_fusion.5
  79.1 0.3 convolution_add_fusion.4
  79.5 0.3 convolution_add_fusion.3
  80.1 0.3 convolution_add_fusion.2
  80.5 0.3 convolution_add_fusion.1
  80.8 0.3 convolution_add_fusion
  81.1 0.8 multiply_convert_fusion
  81.9 464.5 %all-reduce.4.cloned.1.call-done = f32[27,128,128]{2,1,0:T(8,128)} async-done(((f32[27,128,128]{2,1,0:T(8,128)}), f32[27,128,128]{2,1,0:T(8,128)}) %all-reduce.4.cloned.1.call-update) | async-done | bytes 1769488 | tf_op jit(solution)/shard_map/psum | solution.py:99
  546.5 2.9 broadcast_multiply_fusion
  (113 shorter events, 2.1 us)
Async XLA Ops:
  7.2 16.3 %copy-start = (bf16[27,128,128]{2,1,0:T(8,128)(2,1)S(1)}, bf16[27,128,128]{2,1,0:T(8,128)(2,1)}, u32[]{:S(2)}) copy-start(bf16[27,128,128]{2,1,0:T(8,128)(2,1)} %param.6) | copy-start | bytes 2654212
  7.2 539.3 %all-reduce.4.cloned.1.call-start = ((), (), s32[]{:S(2)}) async-start(), calls=%async_computation | async-start | bytes 3538944 | tf_op jit(solution)/shard_map/psum | solution.py:99
  9.8 15.8 %collective-permute-start.5 = (bf16[1,8,8,128]{3,2,1,0:T(8,128)(2,1)S(1)}, bf16[1,8,8,128]{3,2,1,0:T(8,128)(2,1)S(1)}, u32[]{:S(2)}, u32[]{:S(2)}) collective-permute-start(bf16[1,8,8,128]{3,2,1,0:T(8,128)(2,1)S(1)} %get-tuple-element.81), channel_id=1, source_target_pairs={{8,0},{16,8},{24,16},{32,24},{40,32},{48,40},{56,48},{64,56},{72,6... | collective-permute-start | bytes 49160 | tf_op jit(solution)/shard_map/ppermute | solution.py:17
  11.1 14.5 %collective-permute-start.4 = (bf16[1,8,8,128]{3,2,1,0:T(8,128)(2,1)S(1)}, bf16[1,8,8,128]{3,2,1,0:T(8,128)(2,1)S(1)}, u32[]{:S(2)}, u32[]{:S(2)}) collective-permute-start(bf16[1,8,8,128]{3,2,1,0:T(8,128)(2,1)S(1)} %get-tuple-element.80), channel_id=1, source_target_pairs={{0,8},{8,16},{16,24},{24,32},{32,40},{40,48},{48,56},{56,64},{64,7... | collective-permute-start | bytes 49160 | tf_op jit(solution)/shard_map/ppermute | solution.py:16
  16.1 20.1 %collective-permute-start.1 = (bf16[1,8,8,128]{3,2,1,0:T(8,128)(2,1)S(1)}, bf16[1,8,8,128]{3,2,1,0:T(8,128)(2,1)S(1)}, u32[]{:S(2)}, u32[]{:S(2)}) collective-permute-start(bf16[1,8,8,128]{3,2,1,0:T(8,128)(2,1)S(1)} %get-tuple-element.86), channel_id=1, source_target_pairs={{8,0},{16,8},{24,16},{32,24},{40,32},{48,40},{56,48},{64,56},{72,6... | collective-permute-start | bytes 49160 | tf_op jit(solution)/shard_map/ppermute | solution.py:17
  17.4 18.8 %collective-permute-start = (bf16[1,8,8,128]{3,2,1,0:T(8,128)(2,1)S(1)}, bf16[1,8,8,128]{3,2,1,0:T(8,128)(2,1)S(1)}, u32[]{:S(2)}, u32[]{:S(2)}) collective-permute-start(bf16[1,8,8,128]{3,2,1,0:T(8,128)(2,1)S(1)} %get-tuple-element.85), channel_id=1, source_target_pairs={{0,8},{8,16},{16,24},{24,32},{32,40},{40,48},{48,56},{56,64},{64,7... | collective-permute-start | bytes 49160 | tf_op jit(solution)/shard_map/ppermute | solution.py:16
  25.5 18.0 %copy-start.41 = (bf16[1,8,8,128]{3,2,1,0:T(8,128)(2,1)}, bf16[1,8,8,128]{3,2,1,0:T(8,128)(2,1)S(1)}, u32[]{:S(2)}) copy-start(bf16[1,8,8,128]{3,2,1,0:T(8,128)(2,1)S(1)} %collective-permute-done.4) | copy-start | bytes 49156
  25.6 16.3 %collective-permute-start.7 = (bf16[10,1,8,128]{3,2,1,0:T(8,128)(2,1)S(1)}, bf16[10,1,8,128]{3,2,1,0:T(8,128)(2,1)S(1)}, u32[]{:S(2)}, u32[]{:S(2)}) collective-permute-start(bf16[10,1,8,128]{3,2,1,0:T(8,128)(2,1)S(1)} %get-tuple-element.72), channel_id=1, source_target_pairs={{1,0},{2,1},{3,2},{4,3},{5,4},{6,5},{7,6},{9,8},{10,9},{11,10},{12... | collective-permute-start | bytes 61448 | tf_op jit(solution)/shard_map/ppermute | solution.py:17
  34.3 7.6 %collective-permute-start.6 = (bf16[10,1,8,128]{3,2,1,0:T(8,128)(2,1)S(1)}, bf16[10,1,8,128]{3,2,1,0:T(8,128)(2,1)S(1)}, u32[]{:S(2)}, u32[]{:S(2)}) collective-permute-start(bf16[10,1,8,128]{3,2,1,0:T(8,128)(2,1)S(1)} %get-tuple-element.71), channel_id=1, source_target_pairs={{0,1},{1,2},{2,3},{3,4},{4,5},{5,6},{6,7},{8,9},{9,10},{10,11},{11... | collective-permute-start | bytes 61448 | tf_op jit(solution)/shard_map/ppermute | solution.py:16
  36.2 10.5 %copy-start.43 = (bf16[1,8,8,128]{3,2,1,0:T(8,128)(2,1)}, bf16[1,8,8,128]{3,2,1,0:T(8,128)(2,1)S(1)}, u32[]{:S(2)}) copy-start(bf16[1,8,8,128]{3,2,1,0:T(8,128)(2,1)S(1)} %collective-permute-done.1) | copy-start | bytes 49156
  36.3 10.4 %copy-start.44 = (bf16[1,8,8,128]{3,2,1,0:T(8,128)(2,1)}, bf16[1,8,8,128]{3,2,1,0:T(8,128)(2,1)S(1)}, u32[]{:S(2)}) copy-start(bf16[1,8,8,128]{3,2,1,0:T(8,128)(2,1)S(1)} %collective-permute-done) | copy-start | bytes 49156
  36.3 9.0 %collective-permute-start.3 = (bf16[10,1,8,128]{3,2,1,0:T(8,128)(2,1)S(1)}, bf16[10,1,8,128]{3,2,1,0:T(8,128)(2,1)S(1)}, u32[]{:S(2)}, u32[]{:S(2)}) collective-permute-start(bf16[10,1,8,128]{3,2,1,0:T(8,128)(2,1)S(1)} %get-tuple-element.76), channel_id=1, source_target_pairs={{1,0},{2,1},{3,2},{4,3},{5,4},{6,5},{7,6},{9,8},{10,9},{11,10},{12... | collective-permute-start | bytes 61448 | tf_op jit(solution)/shard_map/ppermute | solution.py:17
  38.7 6.6 %collective-permute-start.2 = (bf16[10,1,8,128]{3,2,1,0:T(8,128)(2,1)S(1)}, bf16[10,1,8,128]{3,2,1,0:T(8,128)(2,1)S(1)}, u32[]{:S(2)}, u32[]{:S(2)}) collective-permute-start(bf16[10,1,8,128]{3,2,1,0:T(8,128)(2,1)S(1)} %get-tuple-element.75), channel_id=1, source_target_pairs={{0,1},{1,2},{2,3},{3,4},{4,5},{5,6},{6,7},{8,9},{9,10},{10,11},{11... | collective-permute-start | bytes 61448 | tf_op jit(solution)/shard_map/ppermute | solution.py:16
  60.5 6.0 %copy-start.3 = (bf16[512,384]{0,1:T(8,128)(2,1)S(1)}, bf16[512,384]{0,1:T(8,128)(2,1)}, u32[]{:S(2)}) copy-start(bf16[512,384]{0,1:T(8,128)(2,1)} %copy.20) | copy-start | bytes 1179652
  60.5 7.0 %copy-start.2 = (bf16[512,384]{0,1:T(8,128)(2,1)S(1)}, bf16[512,384]{0,1:T(8,128)(2,1)}, u32[]{:S(2)}) copy-start(bf16[512,384]{0,1:T(8,128)(2,1)} %copy.21) | copy-start | bytes 1179652
  60.5 7.9 %copy-start.1 = (bf16[512,384]{0,1:T(8,128)(2,1)S(1)}, bf16[512,384]{0,1:T(8,128)(2,1)}, u32[]{:S(2)}) copy-start(bf16[512,384]{0,1:T(8,128)(2,1)} %copy.22) | copy-start | bytes 1179652
  62.5 6.8 %copy-start.6 = (bf16[512,384]{0,1:T(8,128)(2,1)S(1)}, bf16[512,384]{0,1:T(8,128)(2,1)}, u32[]{:S(2)}) copy-start(bf16[512,384]{0,1:T(8,128)(2,1)} %copy.23) | copy-start | bytes 1179652
  64.5 5.8 %copy-start.5 = (bf16[512,384]{0,1:T(8,128)(2,1)S(1)}, bf16[512,384]{0,1:T(8,128)(2,1)}, u32[]{:S(2)}) copy-start(bf16[512,384]{0,1:T(8,128)(2,1)} %copy.24) | copy-start | bytes 1179652
  66.5 4.7 copy-start.4
  72.2 2.6 copy-start.40
  72.2 2.9 copy-start.39
  73.5 1.8 copy-start.38
  73.5 2.1 copy-start.37
  75.0 0.9 copy-start.36
  75.3 1.0 copy-start.35
  75.6 0.9 copy-start.34
  75.9 0.9 copy-start.33
  76.2 0.9 copy-start.15
  76.2 1.0 copy-start.16
  76.2 1.0 copy-start.17
  76.2 1.1 copy-start.18
  76.2 1.1 copy-start.19
  76.3 1.2 copy-start.20
  76.3 1.1 copy-start.42
  76.8 1.0 copy-start.32
  77.1 1.0 copy-start.31
  77.4 1.0 copy-start.11
  77.4 1.0 copy-start.12
  77.4 1.0 copy-start.13
  77.4 1.1 copy-start.14
  77.4 1.1 copy-start.23
  77.4 1.2 copy-start.24
  77.8 1.0 copy-start.30
  78.1 1.0 copy-start.29
  78.6 0.9 copy-start.28
  78.7 1.1 copy-start.7
  78.7 1.1 copy-start.8
  78.7 1.1 copy-start.9
  78.8 1.1 copy-start.10
  78.8 1.1 copy-start.21
  78.8 1.1 copy-start.22
  79.1 1.0 copy-start.27
  79.5 1.0 copy-start.26
  79.9 0.9 copy-start.25
  80.0 1.1 copy-start.45
Sparse Core Ops, SparseCore 0:
  72.3 474.1 all-reduce.3
where the time goes:
time: 557 us; the launch traced here: 556 us
  waiting for transfers between devices  465 us (83%)
  starting transfers between devices  28 us (5%)
  local copies, waits for them, and re-layouts  19.6 us (4%)
  matrix products  17.3 us (3%)
  between operations  14.8 us (3%)
  other arithmetic  12 us (2%)
    psum x1, waiting for transfers between devices, shards(): kernel_grad = lax.psum(local_term, ('space', 'tile')) * scale  465 us
    ppermute x4, starting transfers between devices, extended(): before = lax.ppermute(last, axis, up)  14.3 us
    ppermute x4, starting transfers between devices, extended(): after = lax.ppermute(initial, axis, down)  13.7 us
    dot_general x9, matrix products, kernel_terms(): lax.dot_general(stacked, flat_grads, (((0,), (0,)), ((), ())), preferred_...  11.6 us
  transfers between devices with their start and end apart: 9, of which 1 were waited for; matrix products, arithmetic and copies ran while one was open for 3% of the time, Pallas kernels for 0%

commit v1 on v0

v1 whole, which is shorter than its diff:
```python
import functools
import math

import jax
import jax.numpy as jnp
from jax import lax
from jax.experimental import pallas as pl
from jax.experimental.pallas import tpu as pltpu
from jax.sharding import PartitionSpec as P

MESH = pl.DeviceIdType.MESH
CHIPS = (4, 4, 16)
C = 128
DIRS = ((1, 0), (-1, 0), (0, 1), (0, -1), (1, 1), (1, -1), (-1, 1), (-1, -1))
F32 = jnp.float32
BF16 = jnp.bfloat16


def dot(a, b):
    return jnp.dot(a, b, preferred_element_type=F32)


def kernel(
    chips,
    scale,
    feat_hbm,
    occ_hbm,
    kern_hbm,
    cot_hbm,
    out_hbm,
    fgrad_hbm,
    kgrad_hbm,
    feat_v,
    cot_v,
    occ_v,
    kern_v,
    kern_t,
    mask_v,
    features_t,
    padded,
    wide_f,
    wide_g,
    send_face,
    send_corner,
    recv_face,
    recv_corner,
    part,
    pair_buf,
    first_buf,
    second_buf,
    tiles,
    z_buf,
    total,
    out_v,
    fgrad_v,
    in_sem,
    out_sem,
    halo_send,
    halo_recv,
    pair_send,
    pair_recv,
    first_send,
    first_recv,
    second_send,
    second_recv,
    z_send,
    z_recv,
    zg_send,
    zg_recv,
    sg_send,
    sg_recv,
    fg_send,
    fg_recv,
    pg_send,
    pg_recv,
):
    nx, ny, nz = chips
    n_space, n_tile = nx * nz, ny * 2
    space, tile = lax.axis_index("space"), lax.axis_index("tile")
    x, z = space // nz, space % nz
    y, core = tile // 2, tile % 2
    block = C // nx
    block_y = C // ny
    rows = C // (nx * ny)
    per_owner = -(-14 // nz)
    owners = 14 // per_owner

    def at(px, py, pz, pc):
        return {"space": px * nz + pz, "tile": py * 2 + pc}

    def x_peer(d):
        return (x + d) % nx

    def y_peer(d):
        return (y + d) % ny

    def z_peer(d):
        return (z + d) % nz

    def halo_peer(i):
        ds, dt = DIRS[i]
        return {
            "space": (space + ds + n_space) % n_space,
            "tile": (tile + dt + n_tile) % n_tile,
        }

    sibling = at(x, y, z, 1 - core)

    barrier = pltpu.get_barrier_semaphore()

    def greet(device):
        pl.semaphore_signal(barrier, inc=1, device_id=device, device_id_type=MESH)

    for i in range(8):
        greet(halo_peer(i))
    greet(sibling)
    for d in range(1, nx):
        greet(at(x_peer(d), y, z, core))
    for d in range(1, ny):
        greet(at(x, y_peer(d), z, core))

    def greet_z(d, carry):
        greet(at(x, y, z_peer(d), core))
        return carry

    lax.fori_loop(1, nz, greet_z, 0)

    loads = [
        pltpu.make_async_copy(src, dst, in_sem.at[i])
        for i, (src, dst) in enumerate(
            ((occ_hbm, occ_v), (cot_hbm, cot_v), (feat_hbm, feat_v), (kern_hbm, kern_v))
        )
    ]
    for load in loads:
        load.start()

    loads[0].wait()
    cells = occ_v[...].reshape(64, 8).astype(F32).astype(BF16)
    pick = lax.broadcasted_iota(jnp.int32, (512, 64), 0) // 8
    pick = (pick == lax.broadcasted_iota(jnp.int32, (512, 64), 1)).astype(F32)
    spread = dot(pick.astype(BF16), cells)
    own = lax.broadcasted_iota(jnp.int32, (512, 8), 0) % 8
    own = own == lax.broadcasted_iota(jnp.int32, (512, 8), 1)
    column = jnp.sum(jnp.where(own, spread, 0.0), axis=1, keepdims=True)
    mask_v[...] = jnp.broadcast_to(column, (512, C)).reshape(8, 8, 8, C)

    def masked_of(source):
        return source[...].astype(F32) * mask_v[...]

    def fill_halo(which, value):
        edge_x = {1: value[7], -1: value[0]}
        edge_y = {1: value[:, 7], -1: value[:, 0]}
        for i in range(2):
            send_face[which, i] = edge_x[DIRS[i][0]].reshape(64, C).astype(BF16)
        for i in range(2, 4):
            send_face[which, i] = edge_y[DIRS[i][1]].reshape(64, C).astype(BF16)
        for i in range(4, 8):
            corner = edge_x[DIRS[i][0]][7 if DIRS[i][1] == 1 else 0]
            send_corner[which, i - 4] = jnp.concatenate([corner, corner], axis=0).astype(BF16)

    def halo_copies(which):
        copies = []
        for i in range(8):
            if i < 4:
                source, target = send_face.at[which, i], recv_face.at[which, i]
            else:
                source, target = send_corner.at[which, i - 4], recv_corner.at[which, i - 4]
            copies.append(
                pltpu.make_async_remote_copy(
                    src_ref=source,
                    dst_ref=target,
                    send_sem=halo_send.at[which, i],
                    recv_sem=halo_recv.at[which, i],
                    device_id=halo_peer(i),
                    device_id_type=MESH,
                )
            )
        return copies

    inside = {
        (0, 1): (space > 0).astype(F32),
        (0, -1): (space < n_space - 1).astype(F32),
        (1, 1): (tile > 0).astype(F32),
        (1, -1): (tile < n_tile - 1).astype(F32),
    }

    def place_halo(which):
        for i in range(8):
            ds, dt = DIRS[i]
            valid = 1.0
            if ds:
                valid = valid * inside[0, ds]
            if dt:
                valid = valid * inside[1, dt]
            row, col = {1: 0, -1: 9}.get(ds), {1: 0, -1: 9}.get(dt)
            if i < 4:
                value = recv_face[which, i].astype(F32).reshape(8, 8, C) * valid
            else:
                value = recv_corner[which, i - 4].astype(F32)[0:8] * valid
            if ds == 0:
                padded[1:9, col] = value
            elif dt == 0:
                padded[row, 1:9] = value
            else:
                padded[row, col] = value

    z_place = lax.broadcasted_iota(jnp.int32, (10, 8, C), 1)

    def widen(target):
        def slab(i, carry):
            value = padded[i]
            before = jnp.where(z_place == 0, 0.0, pltpu.roll(value, 1, 1))
            after = jnp.where(z_place == 7, 0.0, pltpu.roll(value, 7, 1))
            start = pl.multiple_of(i * 64, 64)
            for sy in range(3):
                for sz, shifted in enumerate((before, value, after)):
                    column = (3 * sy + sz) * C
                    target[pl.ds(start, 64), column : column + C] = (
                        shifted[sy : sy + 8].reshape(64, C).astype(BF16)
                    )
            return carry

        lax.fori_loop(0, 10, slab, 0)

    loads[1].wait()
    masked_grad = masked_of(cot_v)
    padded[1:9, 1:9] = masked_grad
    fill_halo(0, masked_grad)
    pl.semaphore_wait(barrier, 8 + 1 + (nx - 1) + (ny - 1) + (nz - 1))
    halo_g = halo_copies(0)
    for copy in halo_g:
        copy.start()
    loads[2].wait()
    masked = masked_of(feat_v)
    fill_halo(1, masked)
    halo_f = halo_copies(1)
    for copy in halo_f:
        copy.start()
    features_t[...] = jnp.transpose(masked.reshape(512, C)).astype(BF16)

    loads[3].wait()

    def flip(s, carry):
        start = pl.multiple_of(s * C, C)
        kern_t[pl.ds(start, C), :] = jnp.transpose(kern_v[26 - s].astype(F32)).astype(BF16)
        return carry

    lax.fori_loop(0, 27, flip, 0)

    for copy in halo_g:
        copy.wait_recv()
    place_halo(0)
    widen(wide_g)

    def terms(sx, first, last):
        for q in range(first, last, 2):
            end = min(q + 2, last)
            result = dot(features_t[...], wide_g[sx * 64 : sx * 64 + 512, q * C : end * C])
            for j in range(q, end):
                part[26 - (9 * sx + j)] = result[:, (j - q) * C : (j - q + 1) * C]

    mine = core * 14
    theirs = (1 - core) * 14

    def pair_copy(half):
        return pltpu.make_async_remote_copy(
            src_ref=part.at[pl.ds(theirs + 7 * half, 7)],
            dst_ref=pair_buf.at[pl.ds(7 * half, 7)],
            send_sem=pair_send.at[half],
            recv_sem=pair_recv.at[half],
            device_id=sibling,
            device_id_type=MESH,
        )

    part[27] = jnp.zeros((C, C), F32)
    terms(1, 4, 9)
    terms(2, 0, 2)
    terms(0, 0, 6)
    pair = {1: pair_copy(1)}
    pair[1].start()
    terms(2, 2, 9)
    terms(0, 6, 9)
    terms(1, 0, 4)
    pair[0] = pair_copy(0)
    pair[0].start()

    first_size = {0: nx, 1: ny}
    second_size = {0: ny, 1: nx}
    first_block = {0: block, 1: block_y}
    first_place = {0: x * block, 1: y * block_y}
    second_place = {0: x * block + y * rows, 1: y * block_y + x * rows}

    def first_peer(half, d):
        return (x_peer(d), y) if half == 0 else (x, y_peer(d))

    def second_peer(half, d):
        return (x, y_peer(d)) if half == 0 else (x_peer(d), y)

    def first_copies(half):
        copies = []
        for d in range(1, first_size[half]):
            px, py = first_peer(half, d)
            index = px if half == 0 else py
            start = pl.multiple_of(index * first_block[half], 8)
            copies.append(
                pltpu.make_async_remote_copy(
                    src_ref=part.at[pl.ds(mine + 7 * half, 7), pl.ds(start, first_block[half])],
                    dst_ref=first_buf.at[half, d - 1],
                    send_sem=first_send.at[half, d - 1],
                    recv_sem=first_recv.at[half, d - 1],
                    device_id=at(px, py, z, core),
                    device_id_type=MESH,
                )
            )
        return copies

    def second_copies(half):
        copies = []
        base = first_place[half]
        for d in range(1, second_size[half]):
            px, py = second_peer(half, d)
            index = py if half == 0 else px
            start = pl.multiple_of(base + index * rows, 8)
            copies.append(
                pltpu.make_async_remote_copy(
                    src_ref=part.at[pl.ds(mine + 7 * half, 7), pl.ds(start, rows)],
                    dst_ref=second_buf.at[half, d - 1],
                    send_sem=second_send.at[half, d - 1],
                    recv_sem=second_recv.at[half, d - 1],
                    device_id=at(px, py, z, core),
                    device_id_type=MESH,
                )
            )
        return copies

    def add_pair(half):
        pair[half].wait_recv()

        def one(i, carry):
            part[mine + 7 * half + i] = part[mine + 7 * half + i] + pair_buf[7 * half + i]
            return carry

        lax.fori_loop(0, 7, one, 0)

    def add_first(half, copies):
        for copy in copies:
            copy.wait_recv()
        where = pl.ds(pl.multiple_of(first_place[half], 8), first_block[half])
        value = part[pl.ds(mine + 7 * half, 7), where]
        for d in range(1, first_size[half]):
            value = value + first_buf[half, d - 1]
        part[pl.ds(mine + 7 * half, 7), where] = value

    def add_second(half, copies):
        for copy in copies:
            copy.wait_recv()
        where = pl.ds(pl.multiple_of(second_place[half], 8), rows)
        value = part[pl.ds(mine + 7 * half, 7), where]
        for d in range(1, second_size[half]):
            value = value + second_buf[half, d - 1]
        tiles[7 * half : 7 * half + 7] = value

    firsts, seconds = {}, {}
    for half in (1, 0):
        add_pair(half)
        firsts[half] = first_copies(half)
        for copy in firsts[half]:
            copy.start()

    padded[1:9, 1:9] = masked_of(feat_v)
    for copy in halo_f:
        copy.wait_recv()
    place_halo(1)
    widen(wide_f)

    def convolved(wide, weight, target):
        value = dot(wide[0:512, :], weight(0))
        value = value + dot(wide[64:576, :], weight(1))
        value = value + dot(wide[128:640, :], weight(2))
        value = value.reshape(8, 8, 8, C) * mask_v[...]
        target[...] = value.astype(BF16)

    convolved(wide_f, lambda a: kern_v[9 * a : 9 * a + 9].reshape(9 * C, C), out_v)
    out_copy = pltpu.make_async_copy(out_v, out_hbm, out_sem.at[0])
    out_copy.start()

    for half in (1, 0):
        add_first(half, firsts[half])
        seconds[half] = second_copies(half)
        for copy in seconds[half]:
            copy.start()
    for half in (1, 0):
        add_second(half, seconds[half])

    def z_copy(d, target):
        return pltpu.make_async_remote_copy(
            src_ref=tiles.at[pl.ds(target * per_owner, per_owner)],
            dst_ref=z_buf.at[d - 1],
            send_sem=z_send.at[d - 1],
            recv_sem=z_recv.at[d - 1],
            device_id=at(x, y, target, core),
            device_id_type=MESH,
        )

    def z_start(d, carry):
        @pl.when(z_peer(d) < owners)
        def _():
            z_copy(d, z_peer(d)).start()

        return carry

    lax.fori_loop(1, nz, z_start, 0)

    convolved(wide_g, lambda a: kern_t[a * 9 * C : (a + 1) * 9 * C, :], fgrad_v)
    fgrad_copy = pltpu.make_async_copy(fgrad_v, fgrad_hbm, out_sem.at[1])
    fgrad_copy.start()

    def tile_at(owner):
        second_half = (owner * per_owner) // 7
        row = second_place[0] + second_half * (second_place[1] - second_place[0])
        return total.at[pl.ds(mine + owner * per_owner, per_owner), pl.ds(pl.multiple_of(row, 8), rows)]

    def zg_copy(d, owner):
        return pltpu.make_async_remote_copy(
            src_ref=tile_at(owner),
            dst_ref=tile_at(owner),
            send_sem=zg_send.at[d - 1],
            recv_sem=zg_recv.at[d - 1],
            device_id=at(x, y, z_peer(d), core),
            device_id_type=MESH,
        )

    @pl.when(z < owners)
    def _():
        def z_wait(d, carry):
            z_copy(d, z).wait_recv()
            return carry

        lax.fori_loop(1, nz, z_wait, 0)
        value = tiles[pl.ds(z * per_owner, per_owner)]
        for d in range(1, nz):
            value = value + z_buf[d - 1]
        tile_at(z)[...] = value * scale

        def zg_start(d, carry):
            zg_copy(d, z).start()
            return carry

        lax.fori_loop(1, nz, zg_start, 0)

    def zg_wait(d, carry):
        sender = (z - d + nz) % nz

        @pl.when(sender < owners)
        def _():
            zg_copy(d, sender).wait_recv()

        return carry

    lax.fori_loop(1, nz, zg_wait, 0)

    def gathered(half, offsets, row, size):
        return total.at[pl.ds(offsets + 7 * half, 7), pl.ds(pl.multiple_of(row, 8), size)]

    def back(half, level, d, row, size, px, py):
        sends, receives = ((sg_send, sg_recv), (fg_send, fg_recv))[level]
        return pltpu.make_async_remote_copy(
            src_ref=gathered(half, mine, row, size),
            dst_ref=gathered(half, mine, row, size),
            send_sem=sends.at[half, d - 1],
            recv_sem=receives.at[half, d - 1],
            device_id=at(px, py, z, core),
            device_id_type=MESH,
        )

    def pair_back(half, d, offsets, index):
        size = first_block[half]
        return pltpu.make_async_remote_copy(
            src_ref=gathered(half, offsets, index * size, size),
            dst_ref=gathered(half, offsets, index * size, size),
            send_sem=pg_send.at[half, d],
            recv_sem=pg_recv.at[half, d],
            device_id=sibling,
            device_id_type=MESH,
        )

    sent = []
    for half in (1, 0):
        for d in range(1, second_size[half]):
            copy = back(half, 0, d, second_place[half], rows, *second_peer(half, d))
            copy.start()
            sent.append(copy)
    for half in (1, 0):
        mine_at = x if half == 0 else y
        for d in range(1, second_size[half]):
            n = second_size[half]
            from_index = ((y if half == 0 else x) - d + n) % n
            back(half, 0, d, first_place[half] + from_index * rows, rows, x, y).wait_recv()
        for d in range(1, first_size[half]):
            copy = back(half, 1, d, first_place[half], first_block[half], *first_peer(half, d))
            copy.start()
            sent.append(copy)
        copy = pair_back(half, 0, mine, mine_at)
        copy.start()
        sent.append(copy)
    for d in range(1, max(nx, ny)):
        for half in (1, 0):
            n = first_size[half]
            if d < n:
                mine_at = x if half == 0 else y
                from_index = (mine_at - d + n) % n
                back(half, 1, d, from_index * first_block[half], first_block[half], x, y).wait_recv()
                copy = pair_back(half, d, mine, from_index)
                copy.start()
                sent.append(copy)
    for d in range(0, max(nx, ny)):
        for half in (1, 0):
            n = first_size[half]
            if d < n:
                mine_at = x if half == 0 else y
                pair_back(half, d, theirs, (mine_at - d + n) % n).wait_recv()

    kgrad_copy = pltpu.make_async_copy(total.at[0:27], kgrad_hbm, out_sem.at[2])
    kgrad_copy.start()

    for copy in halo_g + halo_f + [pair[0], pair[1]] + sent:
        copy.wait_send()
    for half in (1, 0):
        for copy in firsts[half] + seconds[half]:
            copy.wait_send()

    def z_sent(d, carry):
        @pl.when(z_peer(d) < owners)
        def _():
            z_copy(d, z_peer(d)).wait_send()

        @pl.when(z < owners)
        def _():
            zg_copy(d, z).wait_send()

        return carry

    lax.fori_loop(1, nz, z_sent, 0)
    out_copy.wait()
    fgrad_copy.wait()
    kgrad_copy.wait()


def shards(chips, features, occupancy, weights, cotangent):
    nx, ny, nz = chips
    voxels = 512 * nx * ny * nz * 2
    scale = 1.0 / math.sqrt(voxels)
    rows = C // (nx * ny)
    per_owner = -(-14 // nz)
    most = max(nx, ny)
    dma = pltpu.SemaphoreType.DMA
    return pl.pallas_call(
        functools.partial(kernel, chips, scale),
        out_shape=(
            jax.ShapeDtypeStruct((8, 8, 8, C), BF16),
            jax.ShapeDtypeStruct((8, 8, 8, C), BF16),
            jax.ShapeDtypeStruct((27, C, C), F32),
        ),
        in_specs=[pl.BlockSpec(memory_space=pl.ANY)] * 4,
        out_specs=[pl.BlockSpec(memory_space=pl.ANY)] * 3,
        scratch_shapes=[
            pltpu.VMEM((8, 8, 8, C), BF16),
            pltpu.VMEM((8, 8, 8, C), BF16),
            pltpu.VMEM((8, 8, 8), jnp.int32),
            pltpu.VMEM((27, C, C), BF16),
            pltpu.VMEM((27 * C, C), BF16),
            pltpu.VMEM((8, 8, 8, C), F32),
            pltpu.VMEM((C, 512), BF16),
            pltpu.VMEM((10, 10, 8, C), F32),
            pltpu.VMEM((640, 9 * C), BF16),
            pltpu.VMEM((640, 9 * C), BF16),
            pltpu.VMEM((2, 4, 64, C), BF16),
            pltpu.VMEM((2, 4, 16, C), BF16),
            pltpu.VMEM((2, 4, 64, C), BF16),
            pltpu.VMEM((2, 4, 16, C), BF16),
            pltpu.VMEM((28, C, C), F32),
            pltpu.VMEM((14, C, C), F32),
            pltpu.VMEM((2, most - 1, 7, C // nx, C), F32),
            pltpu.VMEM((2, most - 1, 7, rows, C), F32),
            pltpu.VMEM((14, rows, C), F32),
            pltpu.VMEM((nz - 1, per_owner, rows, C), F32),
            pltpu.VMEM((28, C, C), F32),
            pltpu.VMEM((8, 8, 8, C), BF16),
            pltpu.VMEM((8, 8, 8, C), BF16),
            dma((4,)),
            dma((3,)),
            dma((2, 8)),
            dma((2, 8)),
            dma((2,)),
            dma((2,)),
            dma((2, most - 1)),
            dma((2, most - 1)),
            dma((2, most - 1)),
            dma((2, most - 1)),
            dma((nz - 1,)),
            dma((nz - 1,)),
            dma((nz - 1,)),
            dma((nz - 1,)),
            dma((2, most - 1)),
            dma((2, most - 1)),
            dma((2, most - 1)),
            dma((2, most - 1)),
            dma((2, most)),
            dma((2, most)),
        ],
        compiler_params=pltpu.CompilerParams(
            collective_id=0, has_side_effects=True, vmem_limit_bytes=48 * 1024 * 1024
        ),
        cost_estimate=pl.CostEstimate(
            flops=3 * 2 * 512 * 27 * C * C, bytes_accessed=4_000_000, transcendentals=0
        ),
    )(features, occupancy, weights, cotangent)


def solution(mesh, chips=CHIPS):
    in_specs = (
        P("space", "tile", None, None),
        P("space", "tile", None),
        P(),
        P("space", "tile", None, None),
    )
    out_specs = (P("space", "tile", None, None), P("space", "tile", None, None), P())
    return jax.shard_map(
        functools.partial(shards, chips),
        mesh=mesh,
        in_specs=in_specs,
        out_specs=out_specs,
        check_vma=False,
    )
```

time: 557 us -> 73.2 us (0.13)
  waiting for transfers between devices: 465 us -> 0 us
  Pallas kernels: 0 us -> 66 us
  starting transfers between devices: 28 us -> 0 us
  matrix products: 17.3 us -> 0 us
  between operations: 14.8 us -> 0.65 us
  local copies, waits for them, and re-layouts: 19.6 us -> 6.24 us
  other arithmetic: 12 us -> 0 us
    psum x1 -> x0, waiting for transfers between devices: 465 us -> none  [shards(): kernel_grad = lax.psum(local_term, ('space', 'tile')) * scale]
    pallas_call x0 -> x1, Pallas kernels: none -> 66 us  [shards(): pl.pallas_call(functools.partial(kernel, chips, scale), out_shape=(jax.Sh...]
    ppermute x8 -> x0, starting transfers between devices: 27.9 us -> none  [the longest x4 14.3 us: extended(): before = lax.ppermute(last, axis, up)]
    dot_general x27 -> x0, matrix products: 17.3 us -> none  [the longest x9 11.6 us: kernel_terms(): lax.dot_general(stacked, flat_grads, (((0,), (0,)), ((), ())), preferred_...]
    reshape x9 -> x0, local copies, waits for them, and re-layouts: 8.48 us -> none  [convolve(): stacked = stacked.reshape(size_x * size_y * size_z, -1)]
    slice x10 -> x0, local copies, waits for them, and re-layouts: 7.78 us -> none  [the longest x6 5.82 us: convolve(): padded[shift_x:shift_x + size_x, shift_y:shift_y + size_y, shift_z:shift_...]
    concatenate x12 -> x0, other arithmetic: 5.68 us -> none  [the longest x8 5.08 us: convolve(): jnp.concatenate([padded[shift_x:shift_x + size_x, shift_y:shift_y + size_...]
  transfers between devices with their start and end apart: 9 -> 0, of which waited for: 1 -> 0; matrix products, arithmetic and copies ran while one was open for 3% -> 0% of each run, Pallas kernels for 0% -> 0%
where the time goes in v1:
time: 73.2 us; the launch traced here: 72.9 us
  Pallas kernels  66 us (90%)
  local copies, waits for them, and re-layouts  6.24 us (9%)
    pallas_call x1, Pallas kernels, shards(): pl.pallas_call(functools.partial(kernel, chips, scale), out_shape=(jax.Sh...  66 us
    unnamed x11, local copies, waits for them, and re-layouts  6.24 us

profile of v1, /device:TPU:1, one launch (start us, length us, event | category | flops | bytes accessed | tf_op | source)
XLA Modules:
  0.0 72.9 jit_solution(10938450136494487293)
XLA Ops:
  0.6 0.0 copy-start
  0.6 1.2 %copy-done = bf16[27,128,128]{2,1,0:T(8,128)(2,1)S(1)} copy-done((bf16[27,128,128]{2,1,0:T(8,128)(2,1)S(1)}, bf16[27,128,128]{2,1,0:T(8,128)(2,1)}, u32[]{:S(2)}) %copy-start) | copy-done | bytes 884760
  1.8 0.0 copy-start.1
  1.8 0.9 %copy-done.1 = bf16[8,8,8,128]{3,2,1,0:T(8,128)(2,1)S(1)} copy-done((bf16[8,8,8,128]{3,2,1,0:T(8,128)(2,1)S(1)}, bf16[8,8,8,128]{3,2,1,0:T(8,128)(2,1)}, u32[]{:S(2)}) %copy-start.1) | copy-done | bytes 131096
  2.7 0.0 copy-start.2
  2.7 0.9 %copy-done.2 = bf16[8,8,8,128]{3,2,1,0:T(8,128)(2,1)S(1)} copy-done((bf16[8,8,8,128]{3,2,1,0:T(8,128)(2,1)S(1)}, bf16[8,8,8,128]{3,2,1,0:T(8,128)(2,1)}, u32[]{:S(2)}) %copy-start.2) | copy-done | bytes 131096
  3.6 0.0 copy-start.3
  3.6 0.8 %copy-done.3 = s32[8,8,8]{2,1,0:T(8,128)S(1)} copy-done((s32[8,8,8]{2,1,0:T(8,128)S(1)}, s32[8,8,8]{2,1,0:T(8,128)}, u32[]{:S(2)}) %copy-start.3) | copy-done | bytes 2072
  4.4 66.0 %shard_map.67 = (bf16[8,8,8,128]{3,2,1,0:T(8,128)(2,1)S(1)}, bf16[8,8,8,128]{3,2,1,0:T(8,128)(2,1)S(1)}, f32[27,128,128]{2,1,0:T(8,128)S(1)}) custom-call(bf16[8,8,8,128]{3,2,1,0:T(8,128)(2,1)S(1)} %copy-done.1, s32[8,8,8]{2,1,0:T(8,128)S(1)} %copy-done.3, bf16[27,128,128]{2,1,0:T(8,128)(2,1)S(1)} %copy-done, bf16[8,8,8,128]{3,2,1,0:T(8,128)(2,1)S(1)} %copy-done.2), custom_call_target="tpu_custom_call" | custom-call | flops 1358954496 | bytes 4000000 | tf_op jit(solution)/shard_map/pallas_call | solution.py:557
  70.4 0.7 copy.10
  71.1 0.7 copy.11
  71.7 1.2 %copy.12 = f32[27,128,128]{2,1,0:T(8,128)} copy(f32[27,128,128]{2,1,0:T(8,128)S(1)} %get-tuple-element.8) | data formatting | bytes 3538944
Async XLA Ops:
  0.6 1.2 %copy-start = (bf16[27,128,128]{2,1,0:T(8,128)(2,1)S(1)}, bf16[27,128,128]{2,1,0:T(8,128)(2,1)}, u32[]{:S(2)}) copy-start(bf16[27,128,128]{2,1,0:T(8,128)(2,1)} %kern_hbm.1) | copy-start | bytes 2654212
  1.8 0.9 %copy-start.1 = (bf16[8,8,8,128]{3,2,1,0:T(8,128)(2,1)S(1)}, bf16[8,8,8,128]{3,2,1,0:T(8,128)(2,1)}, u32[]{:S(2)}) copy-start(bf16[8,8,8,128]{3,2,1,0:T(8,128)(2,1)} %feat_hbm.1) | copy-start | bytes 393220
  2.7 0.9 %copy-start.2 = (bf16[8,8,8,128]{3,2,1,0:T(8,128)(2,1)S(1)}, bf16[8,8,8,128]{3,2,1,0:T(8,128)(2,1)}, u32[]{:S(2)}) copy-start(bf16[8,8,8,128]{3,2,1,0:T(8,128)(2,1)} %cot_hbm.1) | copy-start | bytes 393220
  3.6 0.8 %copy-start.3 = (s32[8,8,8]{2,1,0:T(8,128)S(1)}, s32[8,8,8]{2,1,0:T(8,128)}, u32[]{:S(2)}) copy-start(s32[8,8,8]{2,1,0:T(8,128)} %occ_hbm.1) | copy-start | bytes 6148

commit v2 on v1

--- a/solution.py
+++ b/solution.py
@@ -27,9 +27,9 @@
     occ_hbm,
     kern_hbm,
     cot_hbm,
-    out_hbm,
-    fgrad_hbm,
-    kgrad_hbm,
+    out_ref,
+    fgrad_ref,
+    total,
     feat_v,
     cot_v,
     occ_v,
@@ -50,11 +50,12 @@
     second_buf,
     tiles,
     z_buf,
-    total,
+    z_all,
     out_v,
     fgrad_v,
     in_sem,
     out_sem,
+    own_sem,
     halo_send,
     halo_recv,
     pair_send,
@@ -83,7 +84,7 @@
     block_y = C // ny
     rows = C // (nx * ny)
     per_owner = -(-14 // nz)
-    owners = 14 // per_owner
+    slots = nz * per_owner
 
     def at(px, py, pz, pc):
         return {"space": px * nz + pz, "tile": py * 2 + pc}
@@ -238,15 +239,6 @@
         copy.start()
     features_t[...] = jnp.transpose(masked.reshape(512, C)).astype(BF16)
 
-    loads[3].wait()
-
-    def flip(s, carry):
-        start = pl.multiple_of(s * C, C)
-        kern_t[pl.ds(start, C), :] = jnp.transpose(kern_v[26 - s].astype(F32)).astype(BF16)
-        return carry
-
-    lax.fori_loop(0, 27, flip, 0)
-
     for copy in halo_g:
         copy.wait_recv()
     place_halo(0)
@@ -273,6 +265,8 @@
         )
 
     part[27] = jnp.zeros((C, C), F32)
+    if slots > 14:
+        tiles[14:slots] = jnp.zeros((slots - 14, rows, C), F32)
     terms(1, 4, 9)
     terms(2, 0, 2)
     terms(0, 0, 6)
@@ -290,29 +284,51 @@
     first_place = {0: x * block, 1: y * block_y}
     second_place = {0: x * block + y * rows, 1: y * block_y + x * rows}
 
-    def first_peer(half, d):
-        return (x_peer(d), y) if half == 0 else (x, y_peer(d))
+    def first_index(half, d):
+        return x_peer(d + nx) if half == 0 else y_peer(d + ny)
+
+    def first_device(half, d):
+        if half == 0:
+            return at(x_peer(d + nx), y, z, core)
+        return at(x, y_peer(d + ny), z, core)
 
     def second_peer(half, d):
         return (x, y_peer(d)) if half == 0 else (x_peer(d), y)
 
-    def first_copies(half):
-        copies = []
-        for d in range(1, first_size[half]):
-            px, py = first_peer(half, d)
-            index = px if half == 0 else py
-            start = pl.multiple_of(index * first_block[half], 8)
-            copies.append(
-                pltpu.make_async_remote_copy(
-                    src_ref=part.at[pl.ds(mine + 7 * half, 7), pl.ds(start, first_block[half])],
-                    dst_ref=first_buf.at[half, d - 1],
-                    send_sem=first_send.at[half, d - 1],
-                    recv_sem=first_recv.at[half, d - 1],
-                    device_id=at(px, py, z, core),
-                    device_id_type=MESH,
-                )
+    def first_copy(half, slot):
+        sign = 1 if slot % 2 == 0 else -1
+        upper = {0: 0, 1: 1, 2: 1, 3: 0, 4: 0, 5: 1}[slot]
+        target = first_index(half, 2 if slot < 2 else sign)
+        size = first_block[half] // 2
+        start = pl.multiple_of(target * first_block[half] + upper * size, 8)
+        return pltpu.make_async_remote_copy(
+            src_ref=part.at[pl.ds(mine + 7 * half, 7), pl.ds(start, size)],
+            dst_ref=first_buf.at[half, slot, :, 0:size],
+            send_sem=first_send.at[half, slot],
+            recv_sem=first_recv.at[half, slot],
+            device_id=first_device(half, sign),
+            device_id_type=MESH,
+        )
+
+    def first_start(half):
+        ring = first_size[half] > 2
+        firsts[half] = {slot: first_copy(half, slot) for slot in ((0, 1, 2, 3) if ring else (2, 3))}
+        for copy in firsts[half].values():
+            copy.start()
+
+    def first_relay(half):
+        if first_size[half] == 2:
+            return
+        size = first_block[half] // 2
+        for slot in (0, 1):
+            firsts[half][slot].wait_recv()
+            target = first_index(half, 1 if slot == 0 else -1)
+            where = pl.ds(pl.multiple_of(target * first_block[half] + slot * size, 8), size)
+            part[pl.ds(mine + 7 * half, 7), where] = (
+                part[pl.ds(mine + 7 * half, 7), where] + first_buf[half, slot, :, 0:size]
             )
-        return copies
+            firsts[half][slot + 4] = first_copy(half, slot + 4)
+            firsts[half][slot + 4].start()
 
     def second_copies(half):
         copies = []
@@ -342,14 +358,16 @@
 
         lax.fori_loop(0, 7, one, 0)
 
-    def add_first(half, copies):
-        for copy in copies:
-            copy.wait_recv()
-        where = pl.ds(pl.multiple_of(first_place[half], 8), first_block[half])
-        value = part[pl.ds(mine + 7 * half, 7), where]
-        for d in range(1, first_size[half]):
-            value = value + first_buf[half, d - 1]
-        part[pl.ds(mine + 7 * half, 7), where] = value
+    def add_first(half):
+        size = first_block[half] // 2
+        for upper, slots_of in ((0, (3, 4)), (1, (2, 5))):
+            where = pl.ds(pl.multiple_of(first_place[half] + upper * size, 8), size)
+            value = part[pl.ds(mine + 7 * half, 7), where]
+            for slot in slots_of:
+                if slot in firsts[half]:
+                    firsts[half][slot].wait_recv()
+                    value = value + first_buf[half, slot, :, 0:size]
+            part[pl.ds(mine + 7 * half, 7), where] = value
 
     def add_second(half, copies):
         for copy in copies:
@@ -363,15 +381,15 @@
     firsts, seconds = {}, {}
     for half in (1, 0):
         add_pair(half)
-        firsts[half] = first_copies(half)
-        for copy in firsts[half]:
-            copy.start()
+        first_start(half)
 
     padded[1:9, 1:9] = masked_of(feat_v)
     for copy in halo_f:
         copy.wait_recv()
     place_halo(1)
     widen(wide_f)
+    for half in (1, 0):
+        first_relay(half)
 
     def convolved(wide, weight, target):
         value = dot(wide[0:512, :], weight(0))
@@ -380,170 +398,206 @@
         value = value.reshape(8, 8, 8, C) * mask_v[...]
         target[...] = value.astype(BF16)
 
+    loads[3].wait()
     convolved(wide_f, lambda a: kern_v[9 * a : 9 * a + 9].reshape(9 * C, C), out_v)
-    out_copy = pltpu.make_async_copy(out_v, out_hbm, out_sem.at[0])
+    out_copy = pltpu.make_async_copy(out_v, out_ref, out_sem.at[0])
     out_copy.start()
 
     for half in (1, 0):
-        add_first(half, firsts[half])
+        add_first(half)
         seconds[half] = second_copies(half)
         for copy in seconds[half]:
             copy.start()
     for half in (1, 0):
         add_second(half, seconds[half])
 
-    def z_copy(d, target):
+    def z_part(ref, index):
+        return ref.at[pl.ds(index * per_owner, per_owner)]
+
+    def z_copy(d):
         return pltpu.make_async_remote_copy(
-            src_ref=tiles.at[pl.ds(target * per_owner, per_owner)],
-            dst_ref=z_buf.at[d - 1],
-            send_sem=z_send.at[d - 1],
-            recv_sem=z_recv.at[d - 1],
-            device_id=at(x, y, target, core),
-            device_id_type=MESH,
-        )
-
-    def z_start(d, carry):
-        @pl.when(z_peer(d) < owners)
-        def _():
-            z_copy(d, z_peer(d)).start()
-
-        return carry
-
-    lax.fori_loop(1, nz, z_start, 0)
-
-    convolved(wide_g, lambda a: kern_t[a * 9 * C : (a + 1) * 9 * C, :], fgrad_v)
-    fgrad_copy = pltpu.make_async_copy(fgrad_v, fgrad_hbm, out_sem.at[1])
-    fgrad_copy.start()
-
-    def tile_at(owner):
-        second_half = (owner * per_owner) // 7
-        row = second_place[0] + second_half * (second_place[1] - second_place[0])
-        return total.at[pl.ds(mine + owner * per_owner, per_owner), pl.ds(pl.multiple_of(row, 8), rows)]
-
-    def zg_copy(d, owner):
-        return pltpu.make_async_remote_copy(
-            src_ref=tile_at(owner),
-            dst_ref=tile_at(owner),
-            send_sem=zg_send.at[d - 1],
-            recv_sem=zg_recv.at[d - 1],
+            src_ref=z_part(tiles, z_peer(d)),
+            dst_ref=z_part(z_buf, d - 1),
+            send_sem=z_send,
+            recv_sem=z_recv,
             device_id=at(x, y, z_peer(d), core),
             device_id_type=MESH,
         )
 
-    @pl.when(z < owners)
-    def _():
-        def z_wait(d, carry):
-            z_copy(d, z).wait_recv()
-            return carry
-
-        lax.fori_loop(1, nz, z_wait, 0)
-        value = tiles[pl.ds(z * per_owner, per_owner)]
-        for d in range(1, nz):
-            value = value + z_buf[d - 1]
-        tile_at(z)[...] = value * scale
-
-        def zg_start(d, carry):
-            zg_copy(d, z).start()
-            return carry
-
-        lax.fori_loop(1, nz, zg_start, 0)
-
-    def zg_wait(d, carry):
-        sender = (z - d + nz) % nz
-
-        @pl.when(sender < owners)
-        def _():
-            zg_copy(d, sender).wait_recv()
-
+    def zg_copy(d):
+        return pltpu.make_async_remote_copy(
+            src_ref=z_part(z_all, z),
+            dst_ref=z_part(z_all, z),
+            send_sem=zg_send,
+            recv_sem=zg_recv,
+            device_id=at(x, y, z_peer(d), core),
+            device_id_type=MESH,
+        )
+
+    z_whole = pltpu.make_async_remote_copy(
+        src_ref=tiles.at[0 : slots - per_owner],
+        dst_ref=z_buf,
+        send_sem=z_send,
+        recv_sem=z_recv,
+        device_id=sibling,
+        device_id_type=MESH,
+    )
+    zg_whole = pltpu.make_async_remote_copy(
+        src_ref=z_all.at[0 : slots - per_owner],
+        dst_ref=z_all.at[0 : slots - per_owner],
+        send_sem=zg_send,
+        recv_sem=zg_recv,
+        device_id=sibling,
+        device_id_type=MESH,
+    )
+
+    def z_start(d, carry):
+        z_copy(d).start()
         return carry
 
-    lax.fori_loop(1, nz, zg_wait, 0)
+    lax.fori_loop(1, nz, z_start, 0)
+
+    def flip(s, carry):
+        start = pl.multiple_of(s * C, C)
+        kern_t[pl.ds(start, C), :] = jnp.transpose(kern_v[26 - s].astype(F32)).astype(BF16)
+        return carry
+
+    lax.fori_loop(0, 27, flip, 0)
+
+    z_whole.wait_recv()
+    value = tiles[pl.ds(z * per_owner, per_owner)]
+    for d in range(1, nz):
+        value = value + z_buf[(d - 1) * per_owner : d * per_owner]
+    z_all[pl.ds(z * per_owner, per_owner)] = value * scale
+
+    def zg_start(d, carry):
+        zg_copy(d).start()
+        return carry
+
+    lax.fori_loop(1, nz, zg_start, 0)
+
+    for copy in halo_g + halo_f + [pair[0], pair[1]]:
+        copy.wait_send()
+    for half in (1, 0):
+        for copy in list(firsts[half].values()) + seconds[half]:
+            copy.wait_send()
+    z_whole.wait_send()
 
     def gathered(half, offsets, row, size):
         return total.at[pl.ds(offsets + 7 * half, 7), pl.ds(pl.multiple_of(row, 8), size)]
 
-    def back(half, level, d, row, size, px, py):
-        sends, receives = ((sg_send, sg_recv), (fg_send, fg_recv))[level]
+    def second_back(half, d, row):
+        return pltpu.make_async_remote_copy(
+            src_ref=z_all.at[7 * half : 7 * half + 7],
+            dst_ref=gathered(half, mine, row, rows),
+            send_sem=sg_send.at[half, d - 1],
+            recv_sem=sg_recv.at[half, d - 1],
+            device_id=at(*second_peer(half, d), z, core),
+            device_id_type=MESH,
+        )
+
+    def first_back(half, slot, target):
+        sign = 1 if slot % 2 == 0 else -1
+        upper = {0: 0, 1: 1, 2: 1, 3: 0, 4: 0, 5: 1}[slot]
+        size = first_block[half] // 2
+        row = target * first_block[half] + upper * size
         return pltpu.make_async_remote_copy(
             src_ref=gathered(half, mine, row, size),
             dst_ref=gathered(half, mine, row, size),
-            send_sem=sends.at[half, d - 1],
-            recv_sem=receives.at[half, d - 1],
-            device_id=at(px, py, z, core),
+            send_sem=fg_send.at[half, slot],
+            recv_sem=fg_recv.at[half, slot],
+            device_id=first_device(half, sign),
             device_id_type=MESH,
         )
 
-    def pair_back(half, d, offsets, index):
+    def source_of(half, slot):
+        sign = 1 if slot % 2 == 0 else -1
+        return first_index(half, -sign if slot < 4 else 2)
+
+    def pair_back(half, slot, offsets):
         size = first_block[half]
+        if slot == 6:
+            row = first_index(half, 0) * size
+        else:
+            size = size // 2
+            upper = {0: 0, 1: 1, 2: 1, 3: 0, 4: 0, 5: 1}[slot]
+            row = source_of(half, slot) * 2 * size + upper * size
         return pltpu.make_async_remote_copy(
-            src_ref=gathered(half, offsets, index * size, size),
-            dst_ref=gathered(half, offsets, index * size, size),
-            send_sem=pg_send.at[half, d],
-            recv_sem=pg_recv.at[half, d],
+            src_ref=gathered(half, offsets, row, size),
+            dst_ref=gathered(half, offsets, row, size),
+            send_sem=pg_send.at[half, slot],
+            recv_sem=pg_recv.at[half, slot],
             device_id=sibling,
             device_id_type=MESH,
         )
 
+    convolved(wide_g, lambda a: kern_t[a * 9 * C : (a + 1) * 9 * C, :], fgrad_v)
+    fgrad_copy = pltpu.make_async_copy(fgrad_v, fgrad_ref, out_sem.at[1])
+    fgrad_copy.start()
+
+    zg_whole.wait_recv()
     sent = []
+    keeps = {}
     for half in (1, 0):
         for d in range(1, second_size[half]):
-            copy = back(half, 0, d, second_place[half], rows, *second_peer(half, d))
+            copy = second_back(half, d, second_place[half])
             copy.start()
             sent.append(copy)
+        keeps[half] = pltpu.make_async_copy(
+            z_all.at[7 * half : 7 * half + 7],
+            gathered(half, mine, second_place[half], rows),
+            own_sem.at[half],
+        )
+        keeps[half].start()
     for half in (1, 0):
-        mine_at = x if half == 0 else y
-        for d in range(1, second_size[half]):
-            n = second_size[half]
+        n = second_size[half]
+        for d in range(1, n):
             from_index = ((y if half == 0 else x) - d + n) % n
-            back(half, 0, d, first_place[half] + from_index * rows, rows, x, y).wait_recv()
-        for d in range(1, first_size[half]):
-            copy = back(half, 1, d, first_place[half], first_block[half], *first_peer(half, d))
+            second_back(half, d, first_place[half] + from_index * rows).wait_recv()
+        keeps[half].wait()
+        for slot in (0, 1, 2, 3) if first_size[half] > 2 else (0, 1):
+            copy = first_back(half, slot, first_index(half, 0))
             copy.start()
             sent.append(copy)
-        copy = pair_back(half, 0, mine, mine_at)
+        copy = pair_back(half, 6, mine)
         copy.start()
         sent.append(copy)
-    for d in range(1, max(nx, ny)):
+
+    forwarded = []
+    for slot in range(6):
         for half in (1, 0):
-            n = first_size[half]
-            if d < n:
-                mine_at = x if half == 0 else y
-                from_index = (mine_at - d + n) % n
-                back(half, 1, d, from_index * first_block[half], first_block[half], x, y).wait_recv()
-                copy = pair_back(half, d, mine, from_index)
+            if first_size[half] > 2 or slot < 2:
+                first_back(half, slot, source_of(half, slot)).wait_recv()
+                if first_size[half] > 2 and slot < 2:
+                    copy = first_back(half, slot + 4, source_of(half, slot))
+                    copy.start()
+                    sent.append(copy)
+                copy = pair_back(half, slot, mine)
                 copy.start()
-                sent.append(copy)
-    for d in range(0, max(nx, ny)):
-        for half in (1, 0):
-            n = first_size[half]
-            if d < n:
-                mine_at = x if half == 0 else y
-                pair_back(half, d, theirs, (mine_at - d + n) % n).wait_recv()
-
-    kgrad_copy = pltpu.make_async_copy(total.at[0:27], kgrad_hbm, out_sem.at[2])
-    kgrad_copy.start()
-
-    for copy in halo_g + halo_f + [pair[0], pair[1]] + sent:
+                forwarded.append(copy)
+    zg_whole.wait_send()
+    for copy in sent:
         copy.wait_send()
-    for half in (1, 0):
-        for copy in firsts[half] + seconds[half]:
-            copy.wait_send()
-
-    def z_sent(d, carry):
-        @pl.when(z_peer(d) < owners)
-        def _():
-            z_copy(d, z_peer(d)).wait_send()
-
-        @pl.when(z < owners)
-        def _():
-            zg_copy(d, z).wait_send()
-
-        return carry
-
-    lax.fori_loop(1, nz, z_sent, 0)
     out_copy.wait()
     fgrad_copy.wait()
-    kgrad_copy.wait()
+    for slot in (6, 0, 1, 2, 3, 4, 5):
+        for half in (1, 0):
+            if first_size[half] > 2 or slot in (6, 0, 1):
+                pair_back(half, slot, theirs).wait_recv()
+    for copy in forwarded:
+        copy.wait_send()
+
+
+def finish(out_ref, fgrad_ref, kgrad_ref, out_final, fgrad_final, kgrad_final, sem):
+    copies = [
+        pltpu.make_async_copy(kgrad_ref.at[0:27], kgrad_final, sem.at[0]),
+        pltpu.make_async_copy(out_ref, out_final, sem.at[1]),
+        pltpu.make_async_copy(fgrad_ref, fgrad_final, sem.at[2]),
+    ]
+    for copy in copies:
+        copy.start()
+    for copy in copies:
+        copy.wait()
 
 
 def shards(chips, features, occupancy, weights, cotangent):
@@ -554,14 +608,14 @@
     per_owner = -(-14 // nz)
     most = max(nx, ny)
     dma = pltpu.SemaphoreType.DMA
-    return pl.pallas_call(
+    results = pl.pallas_call(
         functools.partial(kernel, chips, scale),
         out_shape=(
             jax.ShapeDtypeStruct((8, 8, 8, C), BF16),
             jax.ShapeDtypeStruct((8, 8, 8, C), BF16),
-            jax.ShapeDtypeStruct((27, C, C), F32),
+            jax.ShapeDtypeStruct((28, C, C), F32),
         ),
-        in_specs=[pl.BlockSpec(memory_space=pl.ANY)] * 4,
+        in_specs=[pl.BlockSpec(memory_space=pltpu.HBM)] * 4,
         out_specs=[pl.BlockSpec(memory_space=pl.ANY)] * 3,
         scratch_shapes=[
             pltpu.VMEM((8, 8, 8, C), BF16),
@@ -580,33 +634,34 @@
             pltpu.VMEM((2, 4, 16, C), BF16),
             pltpu.VMEM((28, C, C), F32),
             pltpu.VMEM((14, C, C), F32),
-            pltpu.VMEM((2, most - 1, 7, C // nx, C), F32),
+            pltpu.VMEM((2, 6, 7, C // (2 * min(nx, ny)), C), F32),
             pltpu.VMEM((2, most - 1, 7, rows, C), F32),
-            pltpu.VMEM((14, rows, C), F32),
-            pltpu.VMEM((nz - 1, per_owner, rows, C), F32),
-            pltpu.VMEM((28, C, C), F32),
+            pltpu.VMEM((nz * per_owner, rows, C), F32),
+            pltpu.VMEM(((nz - 1) * per_owner, rows, C), F32),
+            pltpu.VMEM((nz * per_owner, rows, C), F32),
             pltpu.VMEM((8, 8, 8, C), BF16),
             pltpu.VMEM((8, 8, 8, C), BF16),
             dma((4,)),
-            dma((3,)),
+            dma((2,)),
+            dma((2,)),
             dma((2, 8)),
             dma((2, 8)),
             dma((2,)),
             dma((2,)),
+            dma((2, 6)),
+            dma((2, 6)),
             dma((2, most - 1)),
             dma((2, most - 1)),
+            dma,
+            dma,
+            dma,
+            dma,
             dma((2, most - 1)),
             dma((2, most - 1)),
-            dma((nz - 1,)),
-            dma((nz - 1,)),
-            dma((nz - 1,)),
-            dma((nz - 1,)),
-            dma((2, most - 1)),
-            dma((2, most - 1)),
-            dma((2, most - 1)),
-            dma((2, most - 1)),
-            dma((2, most)),
-            dma((2, most)),
+            dma((2, 6)),
+            dma((2, 6)),
+            dma((2, 7)),
+            dma((2, 7)),
         ],
         compiler_params=pltpu.CompilerParams(
             collective_id=0, has_side_effects=True, vmem_limit_bytes=48 * 1024 * 1024
@@ -614,7 +669,18 @@
         cost_estimate=pl.CostEstimate(
             flops=3 * 2 * 512 * 27 * C * C, bytes_accessed=4_000_000, transcendentals=0
         ),
-    )(features, occupancy, weights, cotangent)
+    )(*(pltpu.with_memory_space_constraint(a, pltpu.HBM) for a in (features, occupancy, weights, cotangent)))
+    return pl.pallas_call(
+        finish,
+        out_shape=(
+            jax.ShapeDtypeStruct((8, 8, 8, C), BF16),
+            jax.ShapeDtypeStruct((8, 8, 8, C), BF16),
+            jax.ShapeDtypeStruct((27, C, C), F32),
+        ),
+        in_specs=[pl.BlockSpec(memory_space=pltpu.VMEM)] * 3,
+        out_specs=[pl.BlockSpec(memory_space=pl.ANY)] * 3,
+        scratch_shapes=[dma((3,))],
+    )(*results)
 
 
 def solution(mesh, chips=CHIPS):

time: 73.2 us -> 71.2 us (0.973)
  local copies, waits for them, and re-layouts: 6.24 us -> 2.55 us
  Pallas kernels: 66 us -> 67.8 us
    unnamed x11 -> x6, local copies, waits for them, and re-layouts: 6.24 us -> 2.55 us
    pallas_call x0 -> x1, Pallas kernels: none -> 2.96 us  [shards(): pl.pallas_call(finish, out_shape=(jax.ShapeDtypeStruct((8, 8, 8, C), BF16...]
    pallas_call x1, Pallas kernels: 66 us -> 64.9 us  [shards(): pl.pallas_call(functools.partial(kernel, chips, scale), out_shape=(jax.Sh...]
where the time goes in v2:
time: 71.2 us; the launch traced here: 71 us
  Pallas kernels  67.8 us (95%)
  local copies, waits for them, and re-layouts  2.55 us (4%)
    pallas_call x1, Pallas kernels, shards(): pl.pallas_call(functools.partial(kernel, chips, scale), out_shape=(jax.Sh...  64.9 us
    pallas_call x1, Pallas kernels, shards(): pl.pallas_call(finish, out_shape=(jax.ShapeDtypeStruct((8, 8, 8, C), BF16...  2.96 us
    unnamed x6, local copies, waits for them, and re-layouts  2.55 us

profile of v2, /device:TPU:1, one launch (start us, length us, event | category | flops | bytes accessed | tf_op | source)
XLA Modules:
  0.0 71.0 jit_solution(2690342003021790762)
XLA Ops:
  0.6 64.9 %shard_map.67 = (bf16[8,8,8,128]{3,2,1,0:T(8,128)(2,1)S(1)}, bf16[8,8,8,128]{3,2,1,0:T(8,128)(2,1)S(1)}, f32[28,128,128]{2,1,0:T(8,128)S(1)}) custom-call(bf16[8,8,8,128]{3,2,1,0:T(8,128)(2,1)} %feat_hbm.1, s32[8,8,8]{2,1,0:T(8,128)} %occ_hbm.1, bf16[27,128,128]{2,1,0:T(8,128)(2,1)} %kern_hbm.1, bf16[8,8,8,128]{3,2,1,0:T(8,128)(2,1)} %cot_hbm.1), custom_call_target="tpu_custom_call" | custom-call | flops 1358954496 | bytes 4000000 | tf_op jit(solution)/shard_map/pallas_call | solution.py:611
  65.5 0.0 copy-start
  65.5 1.2 %copy-done = f32[28,128,128]{2,1,0:T(8,128)} copy-done((f32[28,128,128]{2,1,0:T(8,128)}, f32[28,128,128]{2,1,0:T(8,128)S(1)}, u32[]{:S(2)}) %copy-start) | copy-done | bytes 1835032
  66.8 0.0 copy-start.1
  66.8 0.6 copy-done.1
  67.4 0.0 copy-start.2
  67.4 0.6 copy-done.2
  68.1 3.0 %shard_map.68 = (bf16[8,8,8,128]{3,2,1,0:T(8,128)(2,1)}, bf16[8,8,8,128]{3,2,1,0:T(8,128)(2,1)}, f32[27,128,128]{2,1,0:T(8,128)}) custom-call(bf16[8,8,8,128]{3,2,1,0:T(8,128)(2,1)} %copy-done.1, bf16[8,8,8,128]{3,2,1,0:T(8,128)(2,1)} %copy-done.2, f32[28,128,128]{2,1,0:T(8,128)} %copy-done), custom_call_target="tpu_custom_call" | custom-call | tf_op jit(solution)/shard_map/pallas_call | solution.py:673
Async XLA Ops:
  65.5 1.3 %copy-start = (f32[28,128,128]{2,1,0:T(8,128)}, f32[28,128,128]{2,1,0:T(8,128)S(1)}, u32[]{:S(2)}) copy-start(f32[28,128,128]{2,1,0:T(8,128)S(1)} %get-tuple-element.8.kgrad_ref) | copy-start | bytes 5505028
  66.8 0.6 copy-start.1
  67.4 0.7 copy-start.2

commit v3 on v2

--- a/solution.py
+++ b/solution.py
@@ -56,6 +56,7 @@
     in_sem,
     out_sem,
     own_sem,
+    known,
     halo_send,
     halo_recv,
     pair_send,
@@ -107,6 +108,15 @@
 
     sibling = at(x, y, z, 1 - core)
 
+    loads = [
+        pltpu.make_async_copy(src, dst, in_sem.at[i])
+        for i, (src, dst) in enumerate(
+            ((occ_hbm, occ_v), (cot_hbm, cot_v), (feat_hbm, feat_v), (kern_hbm, kern_v))
+        )
+    ]
+    for load in loads:
+        load.start()
+
     barrier = pltpu.get_barrier_semaphore()
 
     def greet(device):
@@ -120,20 +130,23 @@
     for d in range(1, ny):
         greet(at(x, y_peer(d), z, core))
 
-    def greet_z(d, carry):
-        greet(at(x, y, z_peer(d), core))
-        return carry
-
-    lax.fori_loop(1, nz, greet_z, 0)
-
-    loads = [
-        pltpu.make_async_copy(src, dst, in_sem.at[i])
-        for i, (src, dst) in enumerate(
-            ((occ_hbm, occ_v), (cot_hbm, cot_v), (feat_hbm, feat_v), (kern_hbm, kern_v))
-        )
-    ]
-    for load in loads:
-        load.start()
+    for d in (1, -1):
+        greet(at(x, y, z_peer(d + nz), core))
+
+    def tell(step):
+        d = 2**step
+        if d < nz // 2:
+            for side in (d, -d):
+                pl.semaphore_signal(
+                    known.at[step],
+                    inc=1,
+                    device_id=at(x, y, z_peer(side + nz), core),
+                    device_id_type=MESH,
+                )
+
+    def hear(step):
+        if 2**step < nz // 2:
+            pl.semaphore_wait(known.at[step], 2)
 
     loads[0].wait()
     cells = occ_v[...].reshape(64, 8).astype(F32).astype(BF16)
@@ -227,16 +240,19 @@
     masked_grad = masked_of(cot_v)
     padded[1:9, 1:9] = masked_grad
     fill_halo(0, masked_grad)
-    pl.semaphore_wait(barrier, 8 + 1 + (nx - 1) + (ny - 1) + (nz - 1))
+    pl.semaphore_wait(barrier, 8 + 1 + (nx - 1) + (ny - 1) + 2)
     halo_g = halo_copies(0)
     for copy in halo_g:
         copy.start()
+    tell(0)
     loads[2].wait()
     masked = masked_of(feat_v)
     fill_halo(1, masked)
     halo_f = halo_copies(1)
     for copy in halo_f:
         copy.start()
+    hear(0)
+    tell(1)
     features_t[...] = jnp.transpose(masked.reshape(512, C)).astype(BF16)
 
     for copy in halo_g:
@@ -263,6 +279,9 @@
             device_id=sibling,
             device_id_type=MESH,
         )
+
+    hear(1)
+    tell(2)
 
     part[27] = jnp.zeros((C, C), F32)
     if slots > 14:
@@ -455,6 +474,7 @@
         z_copy(d).start()
         return carry
 
+    hear(2)
     lax.fori_loop(1, nz, z_start, 0)
 
     def flip(s, carry):
@@ -586,18 +606,6 @@
                 pair_back(half, slot, theirs).wait_recv()
     for copy in forwarded:
         copy.wait_send()
-
-
-def finish(out_ref, fgrad_ref, kgrad_ref, out_final, fgrad_final, kgrad_final, sem):
-    copies = [
-        pltpu.make_async_copy(kgrad_ref.at[0:27], kgrad_final, sem.at[0]),
-        pltpu.make_async_copy(out_ref, out_final, sem.at[1]),
-        pltpu.make_async_copy(fgrad_ref, fgrad_final, sem.at[2]),
-    ]
-    for copy in copies:
-        copy.start()
-    for copy in copies:
-        copy.wait()
 
 
 def shards(chips, features, occupancy, weights, cotangent):
@@ -644,6 +652,7 @@
             dma((4,)),
             dma((2,)),
             dma((2,)),
+            pltpu.SemaphoreType.REGULAR((3,)),
             dma((2, 8)),
             dma((2, 8)),
             dma((2,)),
@@ -670,17 +679,7 @@
             flops=3 * 2 * 512 * 27 * C * C, bytes_accessed=4_000_000, transcendentals=0
         ),
     )(*(pltpu.with_memory_space_constraint(a, pltpu.HBM) for a in (features, occupancy, weights, cotangent)))
-    return pl.pallas_call(
-        finish,
-        out_shape=(
-            jax.ShapeDtypeStruct((8, 8, 8, C), BF16),
-            jax.ShapeDtypeStruct((8, 8, 8, C), BF16),
-            jax.ShapeDtypeStruct((27, C, C), F32),
-        ),
-        in_specs=[pl.BlockSpec(memory_space=pltpu.VMEM)] * 3,
-        out_specs=[pl.BlockSpec(memory_space=pl.ANY)] * 3,
-        scratch_shapes=[dma((3,))],
-    )(*results)
+    return results[0], results[1], results[2][:27]
 
 
 def solution(mesh, chips=CHIPS):

time: 71.2 us -> 65.9 us (0.926)
  Pallas kernels: 67.8 us -> 62.4 us
    pallas_call x1 -> x0, Pallas kernels: 2.96 us -> none  [shards(): pl.pallas_call(finish, out_shape=(jax.ShapeDtypeStruct((8, 8, 8, C), BF16...]
    pallas_call x1, Pallas kernels: 64.9 us -> 62.4 us  [shards(): pl.pallas_call(functools.partial(kernel, chips, scale), out_shape=(jax.Sh...]
    slice x0 -> x1, local copies, waits for them, and re-layouts: none -> 1.4 us  [shards(): return (results[0], results[1], results[2][:27])]
    unnamed x6 -> x2, local copies, waits for them, and re-layouts: 2.55 us -> 1.31 us
where the time goes in v3:
time: 65.9 us; the launch traced here: 65.8 us
  Pallas kernels  62.4 us (95%)
  local copies, waits for them, and re-layouts  2.71 us (4%)
    pallas_call x1, Pallas kernels, shards(): pl.pallas_call(functools.partial(kernel, chips, scale), out_shape=(jax.Sh...  62.4 us
    slice x1, local copies, waits for them, and re-layouts, shards(): return (results[0], results[1], results[2][:27])  1.4 us

profile of v3, /device:TPU:1, one launch (start us, length us, event | category | flops | bytes accessed | tf_op | source)
XLA Modules:
  0.0 65.8 jit_solution(11359300883270240146)
XLA Ops:
  0.6 62.4 %shard_map.67 = (bf16[8,8,8,128]{3,2,1,0:T(8,128)(2,1)S(1)}, bf16[8,8,8,128]{3,2,1,0:T(8,128)(2,1)S(1)}, f32[28,128,128]{2,1,0:T(8,128)S(1)}) custom-call(bf16[8,8,8,128]{3,2,1,0:T(8,128)(2,1)} %feat_hbm.1, s32[8,8,8]{2,1,0:T(8,128)} %occ_hbm.1, bf16[27,128,128]{2,1,0:T(8,128)(2,1)} %kern_hbm.1, bf16[8,8,8,128]{3,2,1,0:T(8,128)(2,1)} %cot_hbm.1), custom_call_target="tpu_custom_call" | custom-call | flops 1358954496 | bytes 4000000 | tf_op jit(solution)/shard_map/pallas_call | solution.py:619
  63.1 1.4 %slice.3 = f32[27,128,128]{2,1,0:T(8,128)} slice(f32[28,128,128]{2,1,0:T(8,128)S(1)} %get-tuple-element.8), slice={[0:27], [0:128], [0:128]} | slice | bytes 3538944 | tf_op jit(solution)/shard_map/slice | solution.py:682
  64.5 0.7 copy.9
  65.1 0.7 copy.10

commit v4 on v3

--- a/solution.py
+++ b/solution.py
@@ -283,19 +283,27 @@
     hear(1)
     tell(2)
 
+    def offset_terms(first):
+        for sx in range(3):
+            inside_sx = [26 - o - 9 * sx for o in range(first, min(first + 7, 27)) if (26 - o) // 9 == sx]
+            if inside_sx:
+                terms(sx, min(inside_sx), max(inside_sx) + 1)
+
+    def for_core(first, second):
+        @pl.when(core == 0)
+        def _():
+            offset_terms(first)
+
+        @pl.when(core == 1)
+        def _():
+            offset_terms(second)
+
     part[27] = jnp.zeros((C, C), F32)
-    if slots > 14:
-        tiles[14:slots] = jnp.zeros((slots - 14, rows, C), F32)
-    terms(1, 4, 9)
-    terms(2, 0, 2)
-    terms(0, 0, 6)
-    pair = {1: pair_copy(1)}
-    pair[1].start()
-    terms(2, 2, 9)
-    terms(0, 6, 9)
-    terms(1, 0, 4)
-    pair[0] = pair_copy(0)
-    pair[0].start()
+    pair = {}
+    for half in (1, 0):
+        for_core(14 + 7 * half, 7 * half)
+        pair[half] = pair_copy(half)
+        pair[half].start()
 
     first_size = {0: nx, 1: ny}
     second_size = {0: ny, 1: nx}
@@ -395,10 +403,12 @@
         value = part[pl.ds(mine + 7 * half, 7), where]
         for d in range(1, second_size[half]):
             value = value + second_buf[half, d - 1]
-        tiles[7 * half : 7 * half + 7] = value
+        for i in range(7):
+            tiles[i // per_owner, half, i % per_owner] = value[i]
 
     firsts, seconds = {}, {}
     for half in (1, 0):
+        for_core(7 * half, 14 + 7 * half)
         add_pair(half)
         first_start(half)
 
@@ -427,16 +437,13 @@
         seconds[half] = second_copies(half)
         for copy in seconds[half]:
             copy.start()
-    for half in (1, 0):
-        add_second(half, seconds[half])
-
-    def z_part(ref, index):
-        return ref.at[pl.ds(index * per_owner, per_owner)]
+    def z_part(ref, owner):
+        return ref.at[owner // 2, owner % 2]
 
     def z_copy(d):
         return pltpu.make_async_remote_copy(
             src_ref=z_part(tiles, z_peer(d)),
-            dst_ref=z_part(z_buf, d - 1),
+            dst_ref=z_buf.at[pl.ds((d - 1) * per_owner, per_owner)],
             send_sem=z_send,
             recv_sem=z_recv,
             device_id=at(x, y, z_peer(d), core),
@@ -448,34 +455,51 @@
             src_ref=z_part(z_all, z),
             dst_ref=z_part(z_all, z),
             send_sem=zg_send,
-            recv_sem=zg_recv,
+            recv_sem=zg_recv.at[z % 2],
             device_id=at(x, y, z_peer(d), core),
             device_id_type=MESH,
         )
 
-    z_whole = pltpu.make_async_remote_copy(
-        src_ref=tiles.at[0 : slots - per_owner],
-        dst_ref=z_buf,
-        send_sem=z_send,
-        recv_sem=z_recv,
-        device_id=sibling,
-        device_id_type=MESH,
-    )
-    zg_whole = pltpu.make_async_remote_copy(
-        src_ref=z_all.at[0 : slots - per_owner],
-        dst_ref=z_all.at[0 : slots - per_owner],
-        send_sem=zg_send,
-        recv_sem=zg_recv,
-        device_id=sibling,
-        device_id_type=MESH,
-    )
-
-    def z_start(d, carry):
-        z_copy(d).start()
-        return carry
+    def z_bytes(count, sends, receives):
+        return pltpu.make_async_remote_copy(
+            src_ref=z_buf.at[0 : count * per_owner],
+            dst_ref=z_buf.at[0 : count * per_owner],
+            send_sem=sends,
+            recv_sem=receives,
+            device_id=sibling,
+            device_id_type=MESH,
+        )
+
+    z_whole = z_bytes(nz - 1, z_send, z_recv)
+    zg_whole = z_bytes(nz - 1, zg_send, zg_recv.at[0])
+
+    def zg_arrived(half):
+        @pl.when(z % 2 != half)
+        def _():
+            z_bytes(nz // 2, zg_send, zg_recv.at[half]).wait_recv()
+
+        if nz > 2:
+
+            @pl.when(z % 2 == half)
+            def _():
+                z_bytes(nz // 2 - 1, zg_send, zg_recv.at[half]).wait_recv()
 
     hear(2)
-    lax.fori_loop(1, nz, z_start, 0)
+    if slots > 14:
+        tiles[nz // 2 - 1] = jnp.zeros((2, per_owner, rows, C), F32)
+    for half in (1, 0):
+        add_second(half, seconds[half])
+
+        def z_start(k, carry):
+            d = 2 * k + (z + half) % 2
+
+            @pl.when(d > 0)
+            def _():
+                z_copy(d).start()
+
+            return carry
+
+        lax.fori_loop(0, nz // 2, z_start, 0)
 
     def flip(s, carry):
         start = pl.multiple_of(s * C, C)
@@ -485,10 +509,10 @@
     lax.fori_loop(0, 27, flip, 0)
 
     z_whole.wait_recv()
-    value = tiles[pl.ds(z * per_owner, per_owner)]
+    value = tiles[z // 2, z % 2]
     for d in range(1, nz):
         value = value + z_buf[(d - 1) * per_owner : d * per_owner]
-    z_all[pl.ds(z * per_owner, per_owner)] = value * scale
+    z_all[z // 2, z % 2] = value * scale
 
     def zg_start(d, carry):
         zg_copy(d).start()
@@ -506,9 +530,12 @@
     def gathered(half, offsets, row, size):
         return total.at[pl.ds(offsets + 7 * half, 7), pl.ds(pl.multiple_of(row, 8), size)]
 
+    def z_half(half):
+        return z_all.at[0:7, half, 0] if per_owner == 1 else z_all.at[0, half]
+
     def second_back(half, d, row):
         return pltpu.make_async_remote_copy(
-            src_ref=z_all.at[7 * half : 7 * half + 7],
+            src_ref=z_half(half),
             dst_ref=gathered(half, mine, row, rows),
             send_sem=sg_send.at[half, d - 1],
             recv_sem=sg_recv.at[half, d - 1],
@@ -555,16 +582,16 @@
     fgrad_copy = pltpu.make_async_copy(fgrad_v, fgrad_ref, out_sem.at[1])
     fgrad_copy.start()
 
-    zg_whole.wait_recv()
     sent = []
     keeps = {}
     for half in (1, 0):
+        zg_arrived(half)
         for d in range(1, second_size[half]):
             copy = second_back(half, d, second_place[half])
             copy.start()
             sent.append(copy)
         keeps[half] = pltpu.make_async_copy(
-            z_all.at[7 * half : 7 * half + 7],
+            z_half(half),
             gathered(half, mine, second_place[half], rows),
             own_sem.at[half],
         )
@@ -644,9 +671,9 @@
             pltpu.VMEM((14, C, C), F32),
             pltpu.VMEM((2, 6, 7, C // (2 * min(nx, ny)), C), F32),
             pltpu.VMEM((2, most - 1, 7, rows, C), F32),
-            pltpu.VMEM((nz * per_owner, rows, C), F32),
+            pltpu.VMEM((nz // 2, 2, per_owner, rows, C), F32),
             pltpu.VMEM(((nz - 1) * per_owner, rows, C), F32),
-            pltpu.VMEM((nz * per_owner, rows, C), F32),
+            pltpu.VMEM((nz // 2, 2, per_owner, rows, C), F32),
             pltpu.VMEM((8, 8, 8, C), BF16),
             pltpu.VMEM((8, 8, 8, C), BF16),
             dma((4,)),
@@ -664,7 +691,7 @@
             dma,
             dma,
             dma,
-            dma,
+            dma((2,)),
             dma((2, most - 1)),
             dma((2, most - 1)),
             dma((2, 6)),

time: 65.9 us -> 65.1 us (0.988)
  Pallas kernels: 62.4 us -> 61.6 us
    pallas_call x1, Pallas kernels: 62.4 us -> 61.6 us  [shards(): pl.pallas_call(functools.partial(kernel, chips, scale), out_shape=(jax.Sh...]
where the time goes in v4:
time: 65.1 us; the launch traced here: 64.9 us
  Pallas kernels  61.6 us (95%)
  local copies, waits for them, and re-layouts  2.71 us (4%)
    pallas_call x1, Pallas kernels, shards(): pl.pallas_call(functools.partial(kernel, chips, scale), out_shape=(jax.Sh...  61.6 us
    slice x1, local copies, waits for them, and re-layouts, shards(): return (results[0], results[1], results[2][:27])  1.4 us
    unnamed x2, local copies, waits for them, and re-layouts  1.31 us

profile of v4, /device:TPU:1, one launch (start us, length us, event | category | flops | bytes accessed | tf_op | source)
XLA Modules:
  0.0 64.9 jit_solution(3560279932838922754)
XLA Ops:
  0.6 61.6 %shard_map.67 = (bf16[8,8,8,128]{3,2,1,0:T(8,128)(2,1)S(1)}, bf16[8,8,8,128]{3,2,1,0:T(8,128)(2,1)S(1)}, f32[28,128,128]{2,1,0:T(8,128)S(1)}) custom-call(bf16[8,8,8,128]{3,2,1,0:T(8,128)(2,1)} %feat_hbm.1, s32[8,8,8]{2,1,0:T(8,128)} %occ_hbm.1, bf16[27,128,128]{2,1,0:T(8,128)(2,1)} %kern_hbm.1, bf16[8,8,8,128]{3,2,1,0:T(8,128)(2,1)} %cot_hbm.1), custom_call_target="tpu_custom_call" | custom-call | flops 1358954496 | bytes 4000000 | tf_op jit(solution)/shard_map/pallas_call | solution.py:646
  62.2 1.4 %slice.3 = f32[27,128,128]{2,1,0:T(8,128)} slice(f32[28,128,128]{2,1,0:T(8,128)S(1)} %get-tuple-element.8), slice={[0:27], [0:128], [0:128]} | slice | bytes 3538944 | tf_op jit(solution)/shard_map/slice | solution.py:709
  63.6 0.7 %copy.9 = bf16[8,8,8,128]{3,2,1,0:T(8,128)(2,1)} copy(bf16[8,8,8,128]{3,2,1,0:T(8,128)(2,1)S(1)} %get-tuple-element.12) | data formatting | bytes 262144
  64.3 0.7 %copy.10 = bf16[8,8,8,128]{3,2,1,0:T(8,128)(2,1)} copy(bf16[8,8,8,128]{3,2,1,0:T(8,128)(2,1)S(1)} %get-tuple-element.13) | data formatting | bytes 262144

commit v5 on v4

--- a/solution.py
+++ b/solution.py
@@ -44,6 +44,7 @@
     send_corner,
     recv_face,
     recv_corner,
+    acc,
     part,
     pair_buf,
     first_buf,
@@ -183,13 +184,26 @@
                 pltpu.make_async_remote_copy(
                     src_ref=source,
                     dst_ref=target,
-                    send_sem=halo_send.at[which, i],
-                    recv_sem=halo_recv.at[which, i],
+                    send_sem=halo_send.at[which, i // 4],
+                    recv_sem=halo_recv.at[which, i // 4],
                     device_id=halo_peer(i),
                     device_id_type=MESH,
                 )
             )
         return copies
+
+    def halo_whole(which):
+        return [
+            pltpu.make_async_remote_copy(
+                src_ref=source.at[which],
+                dst_ref=target.at[which],
+                send_sem=halo_send.at[which, i],
+                recv_sem=halo_recv.at[which, i],
+                device_id=sibling,
+                device_id_type=MESH,
+            )
+            for i, (source, target) in enumerate(((send_face, recv_face), (send_corner, recv_corner)))
+        ]
 
     inside = {
         (0, 1): (space > 0).astype(F32),
@@ -255,17 +269,22 @@
     tell(1)
     features_t[...] = jnp.transpose(masked.reshape(512, C)).astype(BF16)
 
-    for copy in halo_g:
+    for copy in halo_whole(0):
         copy.wait_recv()
     place_halo(0)
     widen(wide_g)
 
-    def terms(sx, first, last):
-        for q in range(first, last, 2):
-            end = min(q + 2, last)
-            result = dot(features_t[...], wide_g[sx * 64 : sx * 64 + 512, q * C : end * C])
-            for j in range(q, end):
-                part[26 - (9 * sx + j)] = result[:, (j - q) * C : (j - q + 1) * C]
+    def terms(first):
+        def two(i, carry):
+            for half in range(2):
+                offset = first + 7 * half + i
+                shift = (53 - offset) % 27
+                start = pl.multiple_of((shift // 9) * 64, 64)
+                column = pl.multiple_of((shift % 9) * C, C)
+                part[offset] = dot(features_t[...], wide_g[pl.ds(start, 512), pl.ds(column, C)])
+            return carry
+
+        lax.fori_loop(0, 7, two, 0)
 
     mine = core * 14
     theirs = (1 - core) * 14
@@ -283,25 +302,9 @@
     hear(1)
     tell(2)
 
-    def offset_terms(first):
-        for sx in range(3):
-            inside_sx = [26 - o - 9 * sx for o in range(first, min(first + 7, 27)) if (26 - o) // 9 == sx]
-            if inside_sx:
-                terms(sx, min(inside_sx), max(inside_sx) + 1)
-
-    def for_core(first, second):
-        @pl.when(core == 0)
-        def _():
-            offset_terms(first)
-
-        @pl.when(core == 1)
-        def _():
-            offset_terms(second)
-
-    part[27] = jnp.zeros((C, C), F32)
     pair = {}
+    terms(theirs)
     for half in (1, 0):
-        for_core(14 + 7 * half, 7 * half)
         pair[half] = pair_copy(half)
         pair[half].start()
 
@@ -407,13 +410,13 @@
             tiles[i // per_owner, half, i % per_owner] = value[i]
 
     firsts, seconds = {}, {}
+    terms(mine)
     for half in (1, 0):
-        for_core(7 * half, 14 + 7 * half)
         add_pair(half)
         first_start(half)
 
     padded[1:9, 1:9] = masked_of(feat_v)
-    for copy in halo_f:
+    for copy in halo_whole(1):
         copy.wait_recv()
     place_halo(1)
     widen(wide_f)
@@ -421,14 +424,19 @@
         first_relay(half)
 
     def convolved(wide, weight, target):
-        value = dot(wide[0:512, :], weight(0))
-        value = value + dot(wide[64:576, :], weight(1))
-        value = value + dot(wide[128:640, :], weight(2))
-        value = value.reshape(8, 8, 8, C) * mask_v[...]
+        acc[...] = jnp.zeros((512, C), F32)
+
+        def add(a, carry):
+            start = pl.multiple_of(a * 64, 64)
+            acc[...] = acc[...] + dot(wide[pl.ds(start, 512), :], weight(a))
+            return carry
+
+        lax.fori_loop(0, 3, add, 0)
+        value = acc[...].reshape(8, 8, 8, C) * mask_v[...]
         target[...] = value.astype(BF16)
 
     loads[3].wait()
-    convolved(wide_f, lambda a: kern_v[9 * a : 9 * a + 9].reshape(9 * C, C), out_v)
+    convolved(wide_f, lambda a: kern_v[pl.ds(9 * a, 9)].reshape(9 * C, C), out_v)
     out_copy = pltpu.make_async_copy(out_v, out_ref, out_sem.at[0])
     out_copy.start()
 
@@ -520,7 +528,7 @@
 
     lax.fori_loop(1, nz, zg_start, 0)
 
-    for copy in halo_g + halo_f + [pair[0], pair[1]]:
+    for copy in halo_whole(0) + halo_whole(1) + [pair[0], pair[1]]:
         copy.wait_send()
     for half in (1, 0):
         for copy in list(firsts[half].values()) + seconds[half]:
@@ -578,7 +586,7 @@
             device_id_type=MESH,
         )
 
-    convolved(wide_g, lambda a: kern_t[a * 9 * C : (a + 1) * 9 * C, :], fgrad_v)
+    convolved(wide_g, lambda a: kern_t[pl.ds(pl.multiple_of(a * 9 * C, C), 9 * C), :], fgrad_v)
     fgrad_copy = pltpu.make_async_copy(fgrad_v, fgrad_ref, out_sem.at[1])
     fgrad_copy.start()
 
@@ -667,6 +675,7 @@
             pltpu.VMEM((2, 4, 16, C), BF16),
             pltpu.VMEM((2, 4, 64, C), BF16),
             pltpu.VMEM((2, 4, 16, C), BF16),
+            pltpu.VMEM((512, C), F32),
             pltpu.VMEM((28, C, C), F32),
             pltpu.VMEM((14, C, C), F32),
             pltpu.VMEM((2, 6, 7, C // (2 * min(nx, ny)), C), F32),
@@ -680,8 +689,8 @@
             dma((2,)),
             dma((2,)),
             pltpu.SemaphoreType.REGULAR((3,)),
-            dma((2, 8)),
-            dma((2, 8)),
+            dma((2, 2)),
+            dma((2, 2)),
             dma((2,)),
             dma((2,)),
             dma((2, 6)),

time: 65.1 us -> 66.5 us (1.022)
  Pallas kernels: 61.6 us -> 63 us
    pallas_call x1, Pallas kernels: 61.6 us -> 63 us  [shards(): pl.pallas_call(functools.partial(kernel, chips, scale), out_shape=(jax.Sh...]
where the time goes in v5:
time: 66.5 us; the launch traced here: 66.3 us
  Pallas kernels  63 us (95%)
  local copies, waits for them, and re-layouts  2.71 us (4%)
    pallas_call x1, Pallas kernels, shards(): pl.pallas_call(functools.partial(kernel, chips, scale), out_shape=(jax.Sh...  63 us
    slice x1, local copies, waits for them, and re-layouts, shards(): return (results[0], results[1], results[2][:27])  1.4 us

profile of v5, /device:TPU:1, one launch (start us, length us, event | category | flops | bytes accessed | tf_op | source)
XLA Modules:
  0.0 66.3 jit_solution(4924218540218248639)
XLA Ops:
  0.6 63.0 %shard_map.67 = (bf16[8,8,8,128]{3,2,1,0:T(8,128)(2,1)S(1)}, bf16[8,8,8,128]{3,2,1,0:T(8,128)(2,1)S(1)}, f32[28,128,128]{2,1,0:T(8,128)S(1)}) custom-call(bf16[8,8,8,128]{3,2,1,0:T(8,128)(2,1)} %feat_hbm.1, s32[8,8,8]{2,1,0:T(8,128)} %occ_hbm.1, bf16[27,128,128]{2,1,0:T(8,128)(2,1)} %kern_hbm.1, bf16[8,8,8,128]{3,2,1,0:T(8,128)(2,1)} %cot_hbm.1), custom_call_target="tpu_custom_call" | custom-call | flops 1358954496 | bytes 4000000 | tf_op jit(solution)/shard_map/pallas_call | solution.py:654
  63.6 1.4 %slice.3 = f32[27,128,128]{2,1,0:T(8,128)} slice(f32[28,128,128]{2,1,0:T(8,128)S(1)} %get-tuple-element.8), slice={[0:27], [0:128], [0:128]} | slice | bytes 3538944 | tf_op jit(solution)/shard_map/slice | solution.py:718
  65.0 0.7 copy.9
  65.7 0.7 copy.10

commit v6 on v4

--- a/solution.py
+++ b/solution.py
@@ -50,6 +50,7 @@
     second_buf,
     tiles,
     z_buf,
+    z_sum,
     z_all,
     out_v,
     fgrad_v,
@@ -67,6 +68,8 @@
     second_recv,
     z_send,
     z_recv,
+    zs_send,
+    zs_recv,
     zg_send,
     zg_recv,
     sg_send,
@@ -84,8 +87,10 @@
     block = C // nx
     block_y = C // ny
     rows = C // (nx * ny)
-    per_owner = -(-14 // nz)
-    slots = nz * per_owner
+    near = min(4, nz)
+    groups = nz // near
+    per_owner = 16 // near
+    z_group, z_near = z // near, z % near
 
     def at(px, py, pz, pc):
         return {"space": px * nz + pz, "tile": py * 2 + pc}
@@ -403,8 +408,7 @@
         value = part[pl.ds(mine + 7 * half, 7), where]
         for d in range(1, second_size[half]):
             value = value + second_buf[half, d - 1]
-        for i in range(7):
-            tiles[i // per_owner, half, i % per_owner] = value[i]
+        tiles[8 * half : 8 * half + 7] = value
 
     firsts, seconds = {}, {}
     for half in (1, 0):
@@ -438,68 +442,64 @@
         for copy in seconds[half]:
             copy.start()
     def z_part(ref, owner):
-        return ref.at[owner // 2, owner % 2]
+        return ref.at[pl.ds(owner * per_owner, per_owner)]
+
+    def near_device(d):
+        return at(x, y, z_group * near + (z_near + d) % near, core)
 
     def z_copy(d):
         return pltpu.make_async_remote_copy(
-            src_ref=z_part(tiles, z_peer(d)),
-            dst_ref=z_buf.at[pl.ds((d - 1) * per_owner, per_owner)],
+            src_ref=z_part(tiles, (z_near + d) % near),
+            dst_ref=z_part(z_buf, d - 1),
             send_sem=z_send,
             recv_sem=z_recv,
-            device_id=at(x, y, z_peer(d), core),
+            device_id=near_device(d),
+            device_id_type=MESH,
+        )
+
+    def zs_copy(d):
+        return pltpu.make_async_remote_copy(
+            src_ref=z_sum.at[z_group],
+            dst_ref=z_sum.at[z_group],
+            send_sem=zs_send,
+            recv_sem=zs_recv,
+            device_id=at(x, y, (z_group + d) % groups * near + z_near, core),
             device_id_type=MESH,
         )
 
     def zg_copy(d):
         return pltpu.make_async_remote_copy(
-            src_ref=z_part(z_all, z),
-            dst_ref=z_part(z_all, z),
+            src_ref=z_part(z_all, z_near),
+            dst_ref=z_part(z_all, z_near),
             send_sem=zg_send,
-            recv_sem=zg_recv.at[z % 2],
-            device_id=at(x, y, z_peer(d), core),
-            device_id_type=MESH,
-        )
-
-    def z_bytes(count, sends, receives):
-        return pltpu.make_async_remote_copy(
-            src_ref=z_buf.at[0 : count * per_owner],
-            dst_ref=z_buf.at[0 : count * per_owner],
+            recv_sem=zg_recv,
+            device_id=near_device(d),
+            device_id_type=MESH,
+        )
+
+    def whole(ref, sends, receives):
+        return pltpu.make_async_remote_copy(
+            src_ref=ref,
+            dst_ref=ref,
             send_sem=sends,
             recv_sem=receives,
             device_id=sibling,
             device_id_type=MESH,
         )
 
-    z_whole = z_bytes(nz - 1, z_send, z_recv)
-    zg_whole = z_bytes(nz - 1, zg_send, zg_recv.at[0])
-
-    def zg_arrived(half):
-        @pl.when(z % 2 != half)
-        def _():
-            z_bytes(nz // 2, zg_send, zg_recv.at[half]).wait_recv()
-
-        if nz > 2:
-
-            @pl.when(z % 2 == half)
-            def _():
-                z_bytes(nz // 2 - 1, zg_send, zg_recv.at[half]).wait_recv()
+    z_whole = whole(z_buf, z_send, z_recv)
+    zs_whole = whole(z_sum.at[0 : groups - 1], zs_send, zs_recv) if groups > 1 else None
+    zg_whole = whole(z_buf, zg_send, zg_recv)
 
     hear(2)
-    if slots > 14:
-        tiles[nz // 2 - 1] = jnp.zeros((2, per_owner, rows, C), F32)
     for half in (1, 0):
+        tiles[8 * half + 7] = jnp.zeros((rows, C), F32)
         add_second(half, seconds[half])
-
-        def z_start(k, carry):
-            d = 2 * k + (z + half) % 2
-
-            @pl.when(d > 0)
+        for d in range(1, near):
+
+            @pl.when((z_near + d) % near * 2 // near == half)
             def _():
                 z_copy(d).start()
-
-            return carry
-
-        lax.fori_loop(0, nz // 2, z_start, 0)
 
     def flip(s, carry):
         start = pl.multiple_of(s * C, C)
@@ -509,16 +509,12 @@
     lax.fori_loop(0, 27, flip, 0)
 
     z_whole.wait_recv()
-    value = tiles[z // 2, z % 2]
-    for d in range(1, nz):
+    value = tiles[pl.ds(z_near * per_owner, per_owner)]
+    for d in range(1, near):
         value = value + z_buf[(d - 1) * per_owner : d * per_owner]
-    z_all[z // 2, z % 2] = value * scale
-
-    def zg_start(d, carry):
-        zg_copy(d).start()
-        return carry
-
-    lax.fori_loop(1, nz, zg_start, 0)
+    z_sum[z_group] = value
+    for d in range(1, groups):
+        zs_copy(d).start()
 
     for copy in halo_g + halo_f + [pair[0], pair[1]]:
         copy.wait_send()
@@ -527,11 +523,24 @@
             copy.wait_send()
     z_whole.wait_send()
 
+    convolved(wide_g, lambda a: kern_t[a * 9 * C : (a + 1) * 9 * C, :], fgrad_v)
+    fgrad_copy = pltpu.make_async_copy(fgrad_v, fgrad_ref, out_sem.at[1])
+    fgrad_copy.start()
+
+    if groups > 1:
+        zs_whole.wait_recv()
+    value = z_sum[0]
+    for i in range(1, groups):
+        value = value + z_sum[i]
+    z_all[pl.ds(z_near * per_owner, per_owner)] = value * scale
+    for d in range(1, near):
+        zg_copy(d).start()
+
     def gathered(half, offsets, row, size):
         return total.at[pl.ds(offsets + 7 * half, 7), pl.ds(pl.multiple_of(row, 8), size)]
 
     def z_half(half):
-        return z_all.at[0:7, half, 0] if per_owner == 1 else z_all.at[0, half]
+        return z_all.at[8 * half : 8 * half + 7]
 
     def second_back(half, d, row):
         return pltpu.make_async_remote_copy(
@@ -578,14 +587,10 @@
             device_id_type=MESH,
         )
 
-    convolved(wide_g, lambda a: kern_t[a * 9 * C : (a + 1) * 9 * C, :], fgrad_v)
-    fgrad_copy = pltpu.make_async_copy(fgrad_v, fgrad_ref, out_sem.at[1])
-    fgrad_copy.start()
-
     sent = []
     keeps = {}
+    zg_whole.wait_recv()
     for half in (1, 0):
-        zg_arrived(half)
         for d in range(1, second_size[half]):
             copy = second_back(half, d, second_place[half])
             copy.start()
@@ -623,6 +628,8 @@
                 copy.start()
                 forwarded.append(copy)
     zg_whole.wait_send()
+    if groups > 1:
+        zs_whole.wait_send()
     for copy in sent:
         copy.wait_send()
     out_copy.wait()
@@ -640,7 +647,8 @@
     voxels = 512 * nx * ny * nz * 2
     scale = 1.0 / math.sqrt(voxels)
     rows = C // (nx * ny)
-    per_owner = -(-14 // nz)
+    near = min(4, nz)
+    per_owner = 16 // near
     most = max(nx, ny)
     dma = pltpu.SemaphoreType.DMA
     results = pl.pallas_call(
@@ -671,9 +679,10 @@
             pltpu.VMEM((14, C, C), F32),
             pltpu.VMEM((2, 6, 7, C // (2 * min(nx, ny)), C), F32),
             pltpu.VMEM((2, most - 1, 7, rows, C), F32),
-            pltpu.VMEM((nz // 2, 2, per_owner, rows, C), F32),
-            pltpu.VMEM(((nz - 1) * per_owner, rows, C), F32),
-            pltpu.VMEM((nz // 2, 2, per_owner, rows, C), F32),
+            pltpu.VMEM((16, rows, C), F32),
+            pltpu.VMEM(((near - 1) * per_owner, rows, C), F32),
+            pltpu.VMEM((nz // near, per_owner, rows, C), F32),
+            pltpu.VMEM((16, rows, C), F32),
             pltpu.VMEM((8, 8, 8, C), BF16),
             pltpu.VMEM((8, 8, 8, C), BF16),
             dma((4,)),
@@ -691,7 +700,9 @@
             dma,
             dma,
             dma,
-            dma((2,)),
+            dma,
+            dma,
+            dma,
             dma((2, most - 1)),
             dma((2, most - 1)),
             dma((2, 6)),

time: 65.1 us -> 65.2 us (level)
  no operation moved by 1% of the time
where the time goes in v6:
time: 65.2 us; the launch traced here: 65.1 us
  Pallas kernels  61.7 us (95%)
  local copies, waits for them, and re-layouts  2.71 us (4%)
    pallas_call x1, Pallas kernels, shards(): pl.pallas_call(functools.partial(kernel, chips, scale), out_shape=(jax.Sh...  61.7 us
    slice x1, local copies, waits for them, and re-layouts, shards(): return (results[0], results[1], results[2][:27])  1.4 us
    unnamed x2, local copies, waits for them, and re-layouts  1.31 us

profile of v6, /device:TPU:1, one launch (start us, length us, event | category | flops | bytes accessed | tf_op | source)
XLA Modules:
  0.0 65.1 jit_solution(1991942847477562844)
XLA Ops:
  0.6 61.7 %shard_map.67 = (bf16[8,8,8,128]{3,2,1,0:T(8,128)(2,1)S(1)}, bf16[8,8,8,128]{3,2,1,0:T(8,128)(2,1)S(1)}, f32[28,128,128]{2,1,0:T(8,128)S(1)}) custom-call(bf16[8,8,8,128]{3,2,1,0:T(8,128)(2,1)} %feat_hbm.1, s32[8,8,8]{2,1,0:T(8,128)} %occ_hbm.1, bf16[27,128,128]{2,1,0:T(8,128)(2,1)} %kern_hbm.1, bf16[8,8,8,128]{3,2,1,0:T(8,128)(2,1)} %cot_hbm.1), custom_call_target="tpu_custom_call" | custom-call | flops 1358954496 | bytes 4000000 | tf_op jit(solution)/shard_map/pallas_call | solution.py:654
  62.4 1.4 %slice.3 = f32[27,128,128]{2,1,0:T(8,128)} slice(f32[28,128,128]{2,1,0:T(8,128)S(1)} %get-tuple-element.8), slice={[0:27], [0:128], [0:128]} | slice | bytes 3538944 | tf_op jit(solution)/shard_map/slice | solution.py:720
  63.8 0.7 %copy.9 = bf16[8,8,8,128]{3,2,1,0:T(8,128)(2,1)} copy(bf16[8,8,8,128]{3,2,1,0:T(8,128)(2,1)S(1)} %get-tuple-element.12) | data formatting | bytes 262144
  64.4 0.7 %copy.10 = bf16[8,8,8,128]{3,2,1,0:T(8,128)(2,1)} copy(bf16[8,8,8,128]{3,2,1,0:T(8,128)(2,1)S(1)} %get-tuple-element.13) | data formatting | bytes 262144

commit v7 on v6

--- a/solution.py
+++ b/solution.py
@@ -420,9 +420,9 @@
     for copy in halo_f:
         copy.wait_recv()
     place_halo(1)
-    widen(wide_f)
     for half in (1, 0):
         first_relay(half)
+    widen(wide_f)
 
     def convolved(wide, weight, target):
         value = dot(wide[0:512, :], weight(0))
@@ -431,10 +431,13 @@
         value = value.reshape(8, 8, 8, C) * mask_v[...]
         target[...] = value.astype(BF16)
 
-    loads[3].wait()
-    convolved(wide_f, lambda a: kern_v[9 * a : 9 * a + 9].reshape(9 * C, C), out_v)
-    out_copy = pltpu.make_async_copy(out_v, out_ref, out_sem.at[0])
-    out_copy.start()
+    def flip(s, carry):
+        start = pl.multiple_of(s * C, C)
+        kern_t[pl.ds(start, C), :] = jnp.transpose(kern_v[26 - s].astype(F32)).astype(BF16)
+        return carry
+
+    def flips(part_of):
+        lax.fori_loop(9 * part_of, 9 * part_of + 9, flip, 0, unroll=3)
 
     for half in (1, 0):
         add_first(half)
@@ -492,6 +495,8 @@
     zg_whole = whole(z_buf, zg_send, zg_recv)
 
     hear(2)
+    loads[3].wait()
+    flips(0)
     for half in (1, 0):
         tiles[8 * half + 7] = jnp.zeros((rows, C), F32)
         add_second(half, seconds[half])
@@ -501,13 +506,7 @@
             def _():
                 z_copy(d).start()
 
-    def flip(s, carry):
-        start = pl.multiple_of(s * C, C)
-        kern_t[pl.ds(start, C), :] = jnp.transpose(kern_v[26 - s].astype(F32)).astype(BF16)
-        return carry
-
-    lax.fori_loop(0, 27, flip, 0)
-
+    flips(1)
     z_whole.wait_recv()
     value = tiles[pl.ds(z_near * per_owner, per_owner)]
     for d in range(1, near):
@@ -523,9 +522,9 @@
             copy.wait_send()
     z_whole.wait_send()
 
-    convolved(wide_g, lambda a: kern_t[a * 9 * C : (a + 1) * 9 * C, :], fgrad_v)
-    fgrad_copy = pltpu.make_async_copy(fgrad_v, fgrad_ref, out_sem.at[1])
-    fgrad_copy.start()
+    convolved(wide_f, lambda a: kern_v[9 * a : 9 * a + 9].reshape(9 * C, C), out_v)
+    out_copy = pltpu.make_async_copy(out_v, out_ref, out_sem.at[0])
+    out_copy.start()
 
     if groups > 1:
         zs_whole.wait_recv()
@@ -589,6 +588,7 @@
 
     sent = []
     keeps = {}
+    flips(2)
     zg_whole.wait_recv()
     for half in (1, 0):
         for d in range(1, second_size[half]):
@@ -617,6 +617,11 @@
 
     forwarded = []
     for slot in range(6):
+        if slot == 2:
+            convolved(wide_g, lambda a: kern_t[a * 9 * C : (a + 1) * 9 * C, :], fgrad_v)
+            fgrad_copy = pltpu.make_async_copy(fgrad_v, fgrad_ref, out_sem.at[1])
+            fgrad_copy.start()
+
         for half in (1, 0):
             if first_size[half] > 2 or slot < 2:
                 first_back(half, slot, source_of(half, slot)).wait_recv()

time: 65.2 us -> 65.2 us (level)
  no operation moved by 1% of the time
where the time goes in v7:
time: 65.2 us; the launch traced here: 65 us
  Pallas kernels  61.7 us (95%)
  local copies, waits for them, and re-layouts  2.71 us (4%)
    pallas_call x1, Pallas kernels, shards(): pl.pallas_call(functools.partial(kernel, chips, scale), out_shape=(jax.Sh...  61.7 us
    slice x1, local copies, waits for them, and re-layouts, shards(): return (results[0], results[1], results[2][:27])  1.4 us
    unnamed x2, local copies, waits for them, and re-layouts  1.31 us

profile of v7, /device:TPU:1, one launch (start us, length us, event | category | flops | bytes accessed | tf_op | source)
XLA Modules:
  0.0 65.0 jit_solution(17838262286518564242)
XLA Ops:
  0.6 61.7 %shard_map.67 = (bf16[8,8,8,128]{3,2,1,0:T(8,128)(2,1)S(1)}, bf16[8,8,8,128]{3,2,1,0:T(8,128)(2,1)S(1)}, f32[28,128,128]{2,1,0:T(8,128)S(1)}) custom-call(bf16[8,8,8,128]{3,2,1,0:T(8,128)(2,1)} %feat_hbm.1, s32[8,8,8]{2,1,0:T(8,128)} %occ_hbm.1, bf16[27,128,128]{2,1,0:T(8,128)(2,1)} %kern_hbm.1, bf16[8,8,8,128]{3,2,1,0:T(8,128)(2,1)} %cot_hbm.1), custom_call_target="tpu_custom_call" | custom-call | flops 1358954496 | bytes 4000000 | tf_op jit(solution)/shard_map/pallas_call | solution.py:659
  62.3 1.4 %slice.3 = f32[27,128,128]{2,1,0:T(8,128)} slice(f32[28,128,128]{2,1,0:T(8,128)S(1)} %get-tuple-element.8), slice={[0:27], [0:128], [0:128]} | slice | bytes 3538944 | tf_op jit(solution)/shard_map/slice | solution.py:725
  63.7 0.7 %copy.9 = bf16[8,8,8,128]{3,2,1,0:T(8,128)(2,1)} copy(bf16[8,8,8,128]{3,2,1,0:T(8,128)(2,1)S(1)} %get-tuple-element.12) | data formatting | bytes 262144
  64.4 0.7 %copy.10 = bf16[8,8,8,128]{3,2,1,0:T(8,128)(2,1)} copy(bf16[8,8,8,128]{3,2,1,0:T(8,128)(2,1)S(1)} %get-tuple-element.13) | data formatting | bytes 262144

commit v8 on v7

--- a/solution.py
+++ b/solution.py
@@ -327,40 +327,19 @@
     def second_peer(half, d):
         return (x, y_peer(d)) if half == 0 else (x_peer(d), y)
 
-    def first_copy(half, slot):
-        sign = 1 if slot % 2 == 0 else -1
-        upper = {0: 0, 1: 1, 2: 1, 3: 0, 4: 0, 5: 1}[slot]
-        target = first_index(half, 2 if slot < 2 else sign)
-        size = first_block[half] // 2
-        start = pl.multiple_of(target * first_block[half] + upper * size, 8)
-        return pltpu.make_async_remote_copy(
-            src_ref=part.at[pl.ds(mine + 7 * half, 7), pl.ds(start, size)],
-            dst_ref=first_buf.at[half, slot, :, 0:size],
-            send_sem=first_send.at[half, slot],
-            recv_sem=first_recv.at[half, slot],
-            device_id=first_device(half, sign),
-            device_id_type=MESH,
-        )
-
     def first_start(half):
-        ring = first_size[half] > 2
-        firsts[half] = {slot: first_copy(half, slot) for slot in ((0, 1, 2, 3) if ring else (2, 3))}
-        for copy in firsts[half].values():
-            copy.start()
-
-    def first_relay(half):
-        if first_size[half] == 2:
-            return
-        size = first_block[half] // 2
-        for slot in (0, 1):
-            firsts[half][slot].wait_recv()
-            target = first_index(half, 1 if slot == 0 else -1)
-            where = pl.ds(pl.multiple_of(target * first_block[half] + slot * size, 8), size)
-            part[pl.ds(mine + 7 * half, 7), where] = (
-                part[pl.ds(mine + 7 * half, 7), where] + first_buf[half, slot, :, 0:size]
+        size = first_block[half]
+        for d in range(1, first_size[half]):
+            start = pl.multiple_of(first_index(half, d) * size, 8)
+            firsts[half, d] = pltpu.make_async_remote_copy(
+                src_ref=part.at[pl.ds(mine + 7 * half, 7), pl.ds(start, size)],
+                dst_ref=first_buf.at[half, d - 1, :, 0:size],
+                send_sem=first_send.at[half, d - 1],
+                recv_sem=first_recv.at[half, d - 1],
+                device_id=first_device(half, d),
+                device_id_type=MESH,
             )
-            firsts[half][slot + 4] = first_copy(half, slot + 4)
-            firsts[half][slot + 4].start()
+            firsts[half, d].start()
 
     def second_copies(half):
         copies = []
@@ -391,15 +370,13 @@
         lax.fori_loop(0, 7, one, 0)
 
     def add_first(half):
-        size = first_block[half] // 2
-        for upper, slots_of in ((0, (3, 4)), (1, (2, 5))):
-            where = pl.ds(pl.multiple_of(first_place[half] + upper * size, 8), size)
-            value = part[pl.ds(mine + 7 * half, 7), where]
-            for slot in slots_of:
-                if slot in firsts[half]:
-                    firsts[half][slot].wait_recv()
-                    value = value + first_buf[half, slot, :, 0:size]
-            part[pl.ds(mine + 7 * half, 7), where] = value
+        size = first_block[half]
+        where = pl.ds(pl.multiple_of(first_place[half], 8), size)
+        value = part[pl.ds(mine + 7 * half, 7), where]
+        for d in range(1, first_size[half]):
+            firsts[half, d].wait_recv()
+            value = value + first_buf[half, d - 1, :, 0:size]
+        part[pl.ds(mine + 7 * half, 7), where] = value
 
     def add_second(half, copies):
         for copy in copies:
@@ -420,8 +397,6 @@
     for copy in halo_f:
         copy.wait_recv()
     place_halo(1)
-    for half in (1, 0):
-        first_relay(half)
     widen(wide_f)
 
     def convolved(wide, weight, target):
@@ -518,8 +493,10 @@
     for copy in halo_g + halo_f + [pair[0], pair[1]]:
         copy.wait_send()
     for half in (1, 0):
-        for copy in list(firsts[half].values()) + seconds[half]:
+        for copy in seconds[half]:
             copy.wait_send()
+    for copy in firsts.values():
+        copy.wait_send()
     z_whole.wait_send()
 
     convolved(wide_f, lambda a: kern_v[9 * a : 9 * a + 9].reshape(9 * C, C), out_v)
@@ -551,37 +528,25 @@
             device_id_type=MESH,
         )
 
-    def first_back(half, slot, target):
-        sign = 1 if slot % 2 == 0 else -1
-        upper = {0: 0, 1: 1, 2: 1, 3: 0, 4: 0, 5: 1}[slot]
-        size = first_block[half] // 2
-        row = target * first_block[half] + upper * size
+    def first_back(half, d, index):
+        size = first_block[half]
         return pltpu.make_async_remote_copy(
-            src_ref=gathered(half, mine, row, size),
-            dst_ref=gathered(half, mine, row, size),
-            send_sem=fg_send.at[half, slot],
-            recv_sem=fg_recv.at[half, slot],
-            device_id=first_device(half, sign),
+            src_ref=gathered(half, mine, index * size, size),
+            dst_ref=gathered(half, mine, index * size, size),
+            send_sem=fg_send.at[half, d - 1],
+            recv_sem=fg_recv.at[half, d - 1],
+            device_id=first_device(half, d),
             device_id_type=MESH,
         )
 
-    def source_of(half, slot):
-        sign = 1 if slot % 2 == 0 else -1
-        return first_index(half, -sign if slot < 4 else 2)
-
-    def pair_back(half, slot, offsets):
+    def pair_back(half, d, offsets):
         size = first_block[half]
-        if slot == 6:
-            row = first_index(half, 0) * size
-        else:
-            size = size // 2
-            upper = {0: 0, 1: 1, 2: 1, 3: 0, 4: 0, 5: 1}[slot]
-            row = source_of(half, slot) * 2 * size + upper * size
+        row = first_index(half, -d) * size
         return pltpu.make_async_remote_copy(
             src_ref=gathered(half, offsets, row, size),
             dst_ref=gathered(half, offsets, row, size),
-            send_sem=pg_send.at[half, slot],
-            recv_sem=pg_recv.at[half, slot],
+            send_sem=pg_send.at[half, d],
+            recv_sem=pg_recv.at[half, d],
             device_id=sibling,
             device_id_type=MESH,
         )
@@ -607,29 +572,24 @@
             from_index = ((y if half == 0 else x) - d + n) % n
             second_back(half, d, first_place[half] + from_index * rows).wait_recv()
         keeps[half].wait()
-        for slot in (0, 1, 2, 3) if first_size[half] > 2 else (0, 1):
-            copy = first_back(half, slot, first_index(half, 0))
+        for d in range(1, first_size[half]):
+            copy = first_back(half, d, first_index(half, 0))
             copy.start()
             sent.append(copy)
-        copy = pair_back(half, 6, mine)
+        copy = pair_back(half, 0, mine)
         copy.start()
         sent.append(copy)
 
+    convolved(wide_g, lambda a: kern_t[a * 9 * C : (a + 1) * 9 * C, :], fgrad_v)
+    fgrad_copy = pltpu.make_async_copy(fgrad_v, fgrad_ref, out_sem.at[1])
+    fgrad_copy.start()
+
     forwarded = []
-    for slot in range(6):
-        if slot == 2:
-            convolved(wide_g, lambda a: kern_t[a * 9 * C : (a + 1) * 9 * C, :], fgrad_v)
-            fgrad_copy = pltpu.make_async_copy(fgrad_v, fgrad_ref, out_sem.at[1])
-            fgrad_copy.start()
-
+    for d in (1, 3, 2):
         for half in (1, 0):
-            if first_size[half] > 2 or slot < 2:
-                first_back(half, slot, source_of(half, slot)).wait_recv()
-                if first_size[half] > 2 and slot < 2:
-                    copy = first_back(half, slot + 4, source_of(half, slot))
-                    copy.start()
-                    sent.append(copy)
-                copy = pair_back(half, slot, mine)
+            if d < first_size[half]:
+                first_back(half, d, first_index(half, -d)).wait_recv()
+                copy = pair_back(half, d, mine)
                 copy.start()
                 forwarded.append(copy)
     zg_whole.wait_send()
@@ -639,10 +599,10 @@
         copy.wait_send()
     out_copy.wait()
     fgrad_copy.wait()
-    for slot in (6, 0, 1, 2, 3, 4, 5):
+    for d in (0, 1, 3, 2):
         for half in (1, 0):
-            if first_size[half] > 2 or slot in (6, 0, 1):
-                pair_back(half, slot, theirs).wait_recv()
+            if d < first_size[half]:
+                pair_back(half, d, theirs).wait_recv()
     for copy in forwarded:
         copy.wait_send()
 
@@ -682,7 +642,7 @@
             pltpu.VMEM((2, 4, 16, C), BF16),
             pltpu.VMEM((28, C, C), F32),
             pltpu.VMEM((14, C, C), F32),
-            pltpu.VMEM((2, 6, 7, C // (2 * min(nx, ny)), C), F32),
+            pltpu.VMEM((2, most - 1, 7, C // min(nx, ny), C), F32),
             pltpu.VMEM((2, most - 1, 7, rows, C), F32),
             pltpu.VMEM((16, rows, C), F32),
             pltpu.VMEM(((near - 1) * per_owner, rows, C), F32),

time: 65.2 us -> 64.1 us (0.983)
  Pallas kernels: 61.7 us -> 60.6 us
    pallas_call x1, Pallas kernels: 61.7 us -> 60.6 us  [shards(): pl.pallas_call(functools.partial(kernel, chips, scale), out_shape=(jax.Sh...]
where the time goes in v8:
time: 64.1 us; the launch traced here: 64 us
  Pallas kernels  60.6 us (95%)
  local copies, waits for them, and re-layouts  2.71 us (4%)
    pallas_call x1, Pallas kernels, shards(): pl.pallas_call(functools.partial(kernel, chips, scale), out_shape=(jax.Sh...  60.6 us
    slice x1, local copies, waits for them, and re-layouts, shards(): return (results[0], results[1], results[2][:27])  1.4 us
    unnamed x2, local copies, waits for them, and re-layouts  1.31 us

profile of v8, /device:TPU:1, one launch (start us, length us, event | category | flops | bytes accessed | tf_op | source)
XLA Modules:
  0.0 64.0 jit_solution(7569832990922137991)
XLA Ops:
  0.6 60.6 %shard_map.67 = (bf16[8,8,8,128]{3,2,1,0:T(8,128)(2,1)S(1)}, bf16[8,8,8,128]{3,2,1,0:T(8,128)(2,1)S(1)}, f32[28,128,128]{2,1,0:T(8,128)S(1)}) custom-call(bf16[8,8,8,128]{3,2,1,0:T(8,128)(2,1)} %feat_hbm.1, s32[8,8,8]{2,1,0:T(8,128)} %occ_hbm.1, bf16[27,128,128]{2,1,0:T(8,128)(2,1)} %kern_hbm.1, bf16[8,8,8,128]{3,2,1,0:T(8,128)(2,1)} %cot_hbm.1), custom_call_target="tpu_custom_call" | custom-call | flops 1358954496 | bytes 4000000 | tf_op jit(solution)/shard_map/pallas_call | solution.py:619
  61.3 1.4 %slice.3 = f32[27,128,128]{2,1,0:T(8,128)} slice(f32[28,128,128]{2,1,0:T(8,128)S(1)} %get-tuple-element.8), slice={[0:27], [0:128], [0:128]} | slice | bytes 3538944 | tf_op jit(solution)/shard_map/slice | solution.py:685
  62.7 0.7 %copy.9 = bf16[8,8,8,128]{3,2,1,0:T(8,128)(2,1)} copy(bf16[8,8,8,128]{3,2,1,0:T(8,128)(2,1)S(1)} %get-tuple-element.12) | data formatting | bytes 262144
  63.3 0.7 %copy.10 = bf16[8,8,8,128]{3,2,1,0:T(8,128)(2,1)} copy(bf16[8,8,8,128]{3,2,1,0:T(8,128)(2,1)S(1)} %get-tuple-element.13) | data formatting | bytes 262144

commit v9 on v8

--- a/solution.py
+++ b/solution.py
@@ -256,12 +256,12 @@
     halo_f = halo_copies(1)
     for copy in halo_f:
         copy.start()
+    features_t[...] = jnp.transpose(masked.reshape(512, C)).astype(BF16)
+
+    for copy in halo_g:
+        copy.wait_recv()
     hear(0)
     tell(1)
-    features_t[...] = jnp.transpose(masked.reshape(512, C)).astype(BF16)
-
-    for copy in halo_g:
-        copy.wait_recv()
     place_halo(0)
     widen(wide_g)
 
@@ -284,9 +284,6 @@
             device_id=sibling,
             device_id_type=MESH,
         )
-
-    hear(1)
-    tell(2)
 
     def offset_terms(first):
         for sx in range(3):
@@ -390,6 +387,9 @@
     firsts, seconds = {}, {}
     for half in (1, 0):
         for_core(7 * half, 14 + 7 * half)
+        if half == 1:
+            hear(1)
+            tell(2)
         add_pair(half)
         first_start(half)
 

time: 64.1 us -> 64 us (level)
  no operation moved by 1% of the time
where the time goes in v9:
time: 64 us; the launch traced here: 63.9 us
  Pallas kernels  60.5 us (95%)
  local copies, waits for them, and re-layouts  2.71 us (4%)
  between operations  0.64 us (1%)
    pallas_call x1, Pallas kernels, shards(): pl.pallas_call(functools.partial(kernel, chips, scale), out_shape=(jax.Sh...  60.5 us
    slice x1, local copies, waits for them, and re-layouts, shards(): return (results[0], results[1], results[2][:27])  1.4 us
    unnamed x2, local copies, waits for them, and re-layouts  1.31 us

profile of v9, /device:TPU:1, one launch (start us, length us, event | category | flops | bytes accessed | tf_op | source)
XLA Modules:
  0.0 63.9 jit_solution(8176026789602424850)
XLA Ops:
  0.6 60.5 %shard_map.67 = (bf16[8,8,8,128]{3,2,1,0:T(8,128)(2,1)S(1)}, bf16[8,8,8,128]{3,2,1,0:T(8,128)(2,1)S(1)}, f32[28,128,128]{2,1,0:T(8,128)S(1)}) custom-call(bf16[8,8,8,128]{3,2,1,0:T(8,128)(2,1)} %feat_hbm.1, s32[8,8,8]{2,1,0:T(8,128)} %occ_hbm.1, bf16[27,128,128]{2,1,0:T(8,128)(2,1)} %kern_hbm.1, bf16[8,8,8,128]{3,2,1,0:T(8,128)(2,1)} %cot_hbm.1), custom_call_target="tpu_custom_call" | custom-call | flops 1358954496 | bytes 4000000 | tf_op jit(solution)/shard_map/pallas_call | solution.py:619
  61.2 1.4 %slice.3 = f32[27,128,128]{2,1,0:T(8,128)} slice(f32[28,128,128]{2,1,0:T(8,128)S(1)} %get-tuple-element.8), slice={[0:27], [0:128], [0:128]} | slice | bytes 3538944 | tf_op jit(solution)/shard_map/slice | solution.py:685
  62.6 0.7 %copy.9 = bf16[8,8,8,128]{3,2,1,0:T(8,128)(2,1)} copy(bf16[8,8,8,128]{3,2,1,0:T(8,128)(2,1)S(1)} %get-tuple-element.12) | data formatting | bytes 262144
  63.2 0.7 %copy.10 = bf16[8,8,8,128]{3,2,1,0:T(8,128)(2,1)} copy(bf16[8,8,8,128]{3,2,1,0:T(8,128)(2,1)S(1)} %get-tuple-element.13) | data formatting | bytes 262144

commit v10 on v8

--- a/solution.py
+++ b/solution.py
@@ -312,6 +312,7 @@
 
     first_size = {0: nx, 1: ny}
     second_size = {0: ny, 1: nx}
+    first_order = {h: (2, 1, 3) if n == 4 else tuple(range(1, n)) for h, n in first_size.items()}
     first_block = {0: block, 1: block_y}
     first_place = {0: x * block, 1: y * block_y}
     second_place = {0: x * block + y * rows, 1: y * block_y + x * rows}
@@ -329,7 +330,7 @@
 
     def first_start(half):
         size = first_block[half]
-        for d in range(1, first_size[half]):
+        for d in first_order[half]:
             start = pl.multiple_of(first_index(half, d) * size, 8)
             firsts[half, d] = pltpu.make_async_remote_copy(
                 src_ref=part.at[pl.ds(mine + 7 * half, 7), pl.ds(start, size)],
@@ -572,7 +573,7 @@
             from_index = ((y if half == 0 else x) - d + n) % n
             second_back(half, d, first_place[half] + from_index * rows).wait_recv()
         keeps[half].wait()
-        for d in range(1, first_size[half]):
+        for d in first_order[half]:
             copy = first_back(half, d, first_index(half, 0))
             copy.start()
             sent.append(copy)

time: 64.1 us -> 63.7 us (level)
  no operation moved by 1% of the time
where the time goes in v10:
time: 63.7 us; the launch traced here: 63.5 us
  Pallas kernels  60.2 us (95%)
  local copies, waits for them, and re-layouts  2.71 us (4%)
  between operations  0.64 us (1%)
    pallas_call x1, Pallas kernels, shards(): pl.pallas_call(functools.partial(kernel, chips, scale), out_shape=(jax.Sh...  60.2 us
    slice x1, local copies, waits for them, and re-layouts, shards(): return (results[0], results[1], results[2][:27])  1.4 us
    unnamed x2, local copies, waits for them, and re-layouts  1.31 us

profile of v10, /device:TPU:1, one launch (start us, length us, event | category | flops | bytes accessed | tf_op | source)
XLA Modules:
  0.0 63.5 jit_solution(12059864729023300106)
XLA Ops:
  0.6 60.2 %shard_map.67 = (bf16[8,8,8,128]{3,2,1,0:T(8,128)(2,1)S(1)}, bf16[8,8,8,128]{3,2,1,0:T(8,128)(2,1)S(1)}, f32[28,128,128]{2,1,0:T(8,128)S(1)}) custom-call(bf16[8,8,8,128]{3,2,1,0:T(8,128)(2,1)} %feat_hbm.1, s32[8,8,8]{2,1,0:T(8,128)} %occ_hbm.1, bf16[27,128,128]{2,1,0:T(8,128)(2,1)} %kern_hbm.1, bf16[8,8,8,128]{3,2,1,0:T(8,128)(2,1)} %cot_hbm.1), custom_call_target="tpu_custom_call" | custom-call | flops 1358954496 | bytes 4000000 | tf_op jit(solution)/shard_map/pallas_call | solution.py:620
  60.8 1.4 %slice.3 = f32[27,128,128]{2,1,0:T(8,128)} slice(f32[28,128,128]{2,1,0:T(8,128)S(1)} %get-tuple-element.8), slice={[0:27], [0:128], [0:128]} | slice | bytes 3538944 | tf_op jit(solution)/shard_map/slice | solution.py:686
  62.2 0.7 %copy.9 = bf16[8,8,8,128]{3,2,1,0:T(8,128)(2,1)} copy(bf16[8,8,8,128]{3,2,1,0:T(8,128)(2,1)S(1)} %get-tuple-element.12) | data formatting | bytes 262144
  62.9 0.7 %copy.10 = bf16[8,8,8,128]{3,2,1,0:T(8,128)(2,1)} copy(bf16[8,8,8,128]{3,2,1,0:T(8,128)(2,1)S(1)} %get-tuple-element.13) | data formatting | bytes 262144
